TPU v7x, 256 devices: a whole 4x4x8 slice. The times are simulated.
256 devices in a mesh: dom: 64 (over y_hi, x, z), lon: 4 (over y_lo, core).
Axes of the slice: x: 4, y: 4 (y_hi: 2, y_lo: 2; y = y_hi * 2 + y_lo), z: 8, core: 2. Of those that a mesh axis runs over, the one named last changes fastest.
Arguments:
- state: float32 [64, 4, 4, 128, 512], P('dom', None, None, None, 'lon'), may hold values from -6 to 6
- level_thickness: float32 [4, 128, 512], P(None, None, 'lon'), may hold values from 0.2 to 1
- wet_levels: int32 [128, 512], P(None, 'lon'), may hold values from 0 to 4
- ancestors: int32 [64, 8, 1], P('dom', 'lon'), may hold values from 0 to 63
Outputs:
- forecast: float32 [64, 4, 4, 128, 512], P('dom', None, None, None, 'lon')
All inputs are finite; a program needn't handle non-finite values.
Results may differ from a plain program's by a relative error of at most 0.0003.
Values sent between devices are 32-bit elements; how exact they have to be, the bound alone decides.
No kernel may reach another device: no remote copies, remote signals or barrier semaphores. Data moves between devices by JAX's collectives and lax.ppermute only.
A program may use at most 64 MiB of HBM per device.

v0:
```python
import jax
import jax.numpy as jnp
from jax import lax
from jax.sharding import PartitionSpec as P

LEV = 4
TILE = 64
BLEND = 8
STEPS = 3
LAT = 128


time_step = 0.3
gravity = 1.0
drag_rate = 0.05
diffusion = 0.1
vertical_mix = 0.2
coriolis_base = 0.1
coriolis_slope = 0.3


def padded_2(x, sides, width):
    for axis, dim in sides:
        size, length = (lax.axis_size(axis), x.shape[dim])
        up = [(i, (i + 1) % size) for i in range(size)]
        down = [(j, i) for i, j in up]
        last = lax.slice_in_dim(x, length - width, length, axis=dim)
        initial = lax.slice_in_dim(x, 0, width, axis=dim)
        before = lax.ppermute(last, axis, up)
        after = lax.ppermute(initial, axis, down)
        x = jnp.concatenate([before, x, after], axis=dim)
    return x


def trim_cols(array, width):
    return array[..., width : array.shape[-1] - width]


def pad_rows(array):
    return jnp.pad(array, [(0, 0)] * (array.ndim - 2) + [(1, 1), (0, 0)])


def diff_lon(array):
    return 0.5 * (array[..., 2:] - array[..., :-2])


def diff_lat(array):
    padded = pad_rows(array)
    return 0.5 * (padded[..., 2:, :] - padded[..., :-2, :])


def laplace(array):
    padded = pad_rows(array)
    centre = array[..., 1:-1]
    return (
        array[..., 2:]
        + array[..., :-2]
        + padded[..., 2:, 1:-1]
        + padded[..., :-2, 1:-1]
        - 4.0 * centre
    )


def vertical_step(tracer_two, wet_two):
    exchanged = vertical_mix * wet_two[1:] * wet_two[:-1] * (tracer_two[1:] - tracer_two[:-1])
    zero_layer = jnp.zeros_like(tracer_two[:1])
    return (
        tracer_two
        + jnp.concatenate([exchanged, zero_layer], 0)
        - jnp.concatenate([zero_layer, exchanged], 0)
    )


def advance(fields, thickness, coriolis):
    height = fields[0]
    zonal = fields[1]
    meridional = fields[2]
    tracer = fields[3]
    wetness = (thickness > 0).astype(fields.dtype)
    wet_one = trim_cols(wetness, 1)
    zonal_one = wet_one * (
        trim_cols(zonal, 1)
        + time_step
        * (
            coriolis * trim_cols(meridional, 1)
            - gravity * diff_lon(height)
            - drag_rate * trim_cols(zonal, 1)
        )
    )
    merid_one = wet_one * (
        trim_cols(meridional, 1)
        + time_step
        * (
            -coriolis * trim_cols(zonal, 1)
            - gravity * trim_cols(diff_lat(height), 1)
            - drag_rate * trim_cols(meridional, 1)
        )
    )
    depth_one = trim_cols(thickness, 1)
    wet_two = trim_cols(wetness, 2)
    height_two = wet_two * (
        trim_cols(height, 2)
        - time_step
        * (diff_lon(depth_one * zonal_one) + trim_cols(diff_lat(depth_one * merid_one), 1))
    )
    tracer_one = trim_cols(tracer, 1)
    transport = diff_lon(zonal_one * tracer_one) + trim_cols(diff_lat(merid_one * tracer_one), 1)
    tracer_two = wet_two * (
        trim_cols(tracer, 2) - time_step * transport + diffusion * trim_cols(laplace(tracer), 1)
    )
    tracer_two = vertical_step(tracer_two, wet_two)
    return jnp.stack([height_two, trim_cols(zonal_one, 1), trim_cols(merid_one, 1), tracer_two])


def edge_weight(position):
    near_left = position < BLEND
    near_right = position >= TILE - BLEND
    distance = jnp.where(near_left, position, TILE - 1 - position).astype(jnp.float32)
    return jnp.where(near_left | near_right, 0.5 + (distance + 0.5) / (2.0 * BLEND), 1.0)


def column_tables(table, position):
    own = jnp.repeat(table[:, 1:-1], TILE, axis=1)
    left = jnp.repeat(table[:, :-2], TILE, axis=1)
    right = jnp.repeat(table[:, 2:], TILE, axis=1)
    neighbour = jnp.where(position < BLEND, left, jnp.where(position >= TILE - BLEND, right, own))
    return (own, neighbour)


def blend_members(block, own, neighbour, weight):
    sources = jnp.arange(block.shape[0], dtype=jnp.int32)[None, :, None]
    picks = jnp.where(own[:, None, :] == sources, weight, 0.0)
    others = jnp.where(neighbour[:, None, :] == sources, 1.0 - weight, 0.0)
    mixing = picks + others
    return jnp.einsum("osx,sfkrx->ofkrx", mixing, block, precision=lax.Precision.HIGHEST)


def on_device(state, level_thickness, wet_levels, ancestors):
    width = state.shape[-1]
    position = jnp.arange(width) % TILE
    weight = edge_weight(position)
    rimmed = padded_2(ancestors, (("lon", 1),), 1)
    everyone = lax.all_gather(rimmed, "dom", axis=0, tiled=True)
    own, neighbour = column_tables(everyone[:, :, 0], position)
    mask = (jnp.arange(LEV)[:, None, None] < wet_levels[None]).astype(jnp.float32)
    thickness = level_thickness * mask
    mixed = blend_members(
        lax.all_to_all(state, "dom", split_axis=3, concat_axis=0, tiled=True),
        own,
        neighbour,
        weight,
    )
    blended = lax.all_to_all(mixed, "dom", split_axis=0, concat_axis=3, tiled=True)
    fields = blended[0]
    coriolis = (coriolis_base + coriolis_slope * jnp.arange(LAT) / LAT)[:, None].astype(jnp.float32)
    extended = jnp.concatenate([fields, thickness[None]], 0)
    for substep in range(STEPS):
        padded = padded_2(extended, (("lon", 3),), 2)
        fields = advance(padded[:4], padded[4], coriolis)
        extended = jnp.concatenate([fields, thickness[None]], 0)
    return fields[None]


def solution(mesh):
    return jax.shard_map(
        on_device,
        mesh=mesh,
        in_specs=(
            P("dom", None, None, None, "lon"),
            P(None, None, "lon"),
            P(None, "lon"),
            P("dom", "lon", None),
        ),
        out_specs=P("dom", None, None, None, "lon"),
        check_vma=False,
    )
```

profile of v0, /device:TPU:1, one launch (start us, length us, event | category | flops | bytes accessed | tf_op | source)
XLA Modules:
  0.0 300.9 jit_solution(15388926744871958385)
XLA Ops:
  0.0 2.9 copy.16
  2.9 15.2 %all-to-all-start = ((f32[1,4,4,128,128]{4,2,1,0,3:T(4,128)}), f32[1,4,4,128,128]{4,2,1,0,3:T(4,128)S(1)}, u32[]{:S(2)}, u32[]{:S(2)}) async-start(f32[1,4,4,128,128]{4,2,1,0,3:T(4,128)} %copy.16), calls=%async_computation | async-start | bytes 2097152 | tf_op jit(solution)/shard_map/all_to_all | solution.py:148
  18.7 1.2 collective-permute-start
  20.8 2.7 collective-permute-done.1
  23.5 1.3 pad_add_fusion
  24.8 158.9 %all_gather.3 = s32[64,4,1]{1,2,0:T(1,128)S(1)} all-gather(s32[1,4,1]{1,2,0:T(1,128)S(1)} %pad_add_fusion), channel_id=1, replica_groups=mesh['dom'=64,'lon'=4] {'dom'}, dimensions={0}, use_global_device_ids=true | all-gather | bytes 1040 | tf_op jit(solution)/shard_map/all_gather | solution.py:143
  184.2 1.7 copy.18
  185.9 10.6 %fusion.11 = f32[64,4,4,2,128]{0,2,3,1,4:T(4,128)} fusion(f32[1,4,4,64,2,128]{3,2,4,1,5,0:T(4,128)S(1)} %copy.18, f32[128]{0:T(128)S(1)} %get-tuple-element.93, s32[64,128]{0,1:T(8,128)S(1)} %fusion.109, f32[128]{0:T(128)S(1)} %get-tuple-element.92, s32[64,128]{0,1:T(8,128)S(1)} %bitcast.115), kind=kOutput, calls=%fused_computation.16 | convolution fusion | flops 203948032 | bytes 2163712 | tf_op jit(solution)/shard_map/osx,sfkrx->ofkrx/dot_general | solution.py:135
  196.5 3.1 %copy.19 = f32[64,4,4,2,128]{4,2,3,1,0:T(4,128)} copy(f32[64,4,4,2,128]{0,2,3,1,4:T(4,128)} %fusion.11) | data formatting | bytes 2097152 | tf_op jit(solution)/shard_map/osx,sfkrx->ofkrx/transpose | solution.py:135
  199.5 4.8 %all-to-all-start.1 = ((f32[64,4,4,2,128]{4,2,3,1,0:T(4,128)}), f32[64,4,4,2,128]{4,2,3,1,0:T(4,128)S(1)}, u32[]{:S(2)}, u32[]{:S(2)}) async-start(f32[64,4,4,2,128]{4,2,3,1,0:T(4,128)} %copy.19), calls=%async_computation.1 | async-start | bytes 2097152 | tf_op jit(solution)/shard_map/all_to_all | solution.py:153
  204.4 18.9 %all-to-all-done.1 = f32[64,4,4,2,128]{4,2,3,1,0:T(4,128)S(1)} async-done(((f32[64,4,4,2,128]{4,2,3,1,0:T(4,128)}), f32[64,4,4,2,128]{4,2,3,1,0:T(4,128)S(1)}, u32[]{:S(2)}, u32[]{:S(2)}) %all-to-all-start.1) | async-done | bytes 1048608 | tf_op jit(solution)/shard_map/all_to_all | solution.py:153
  223.8 1.5 slice_maximum_fusion
  225.4 1.7 copy.21
  227.1 31.1 %collective-permute-start.2 = (f32[5,4,128,2]{2,1,3,0:T(4,128)S(1)}, f32[5,4,128,2]{2,1,3,0:T(4,128)S(1)}, u32[]{:S(2)}, u32[]{:S(2)}) collective-permute-start(f32[5,4,128,2]{2,1,3,0:T(4,128)S(1)} %copy.21), channel_id=1, source_target_pairs={{0,1},{1,2},{2,3},{3,0},{4,5},{5,6},{6,7},{7,4},{8,9},{9,10},{10,1... | collective-permute-start | bytes 61448 | tf_op jit(solution)/shard_map/ppermute | solution.py:29
  259.5 2.5 collective-permute-done.3
  262.0 1.5 copy.24
  263.5 2.4 pad_maximum_fusion
  266.3 1.5 slice_multiply_fusion.20
  269.9 1.5 fusion.121
  271.4 1.7 copy.25
  274.8 2.3 collective-permute-done.5
  277.1 1.5 copy.28
  278.6 2.4 pad_maximum_fusion.1
  281.3 1.5 slice_multiply_fusion.18
  284.9 1.5 fusion.120
  286.5 1.7 copy.29
  289.9 2.3 collective-permute-done.7
  292.1 1.5 copy.32
  293.7 2.4 pad_maximum_fusion.2
  296.4 1.1 slice_multiply_fusion.1
  298.6 1.0 fusion.66
  299.8 1.0 maximum_bitcast_fusion
  (71 shorter events, 13.4 us)
Async XLA Ops:
  2.9 15.3 %copy-start.2 = (s32[1,2,1]{1,2,0:T(1,128)S(1)}, s32[1,2,1]{1,2,0:T(1,128)}, u32[]{:S(2)}) copy-start(s32[1,2,1]{1,2,0:T(1,128)} %param.7) | copy-start | bytes 28
  2.9 181.3 %all-to-all-start = ((f32[1,4,4,128,128]{4,2,1,0,3:T(4,128)}), f32[1,4,4,128,128]{4,2,1,0,3:T(4,128)S(1)}, u32[]{:S(2)}, u32[]{:S(2)}) async-start(f32[1,4,4,128,128]{4,2,1,0,3:T(4,128)} %copy.16), calls=%async_computation | async-start | bytes 2097152 | tf_op jit(solution)/shard_map/all_to_all | solution.py:148
  18.7 2.0 collective-permute-start
  20.0 3.5 %collective-permute-start.1 = (s32[1,1,1]{1,2,0:T(1,128)}, s32[1,1,1]{1,2,0:T(1,128)}, u32[]{:S(2)}, u32[]{:S(2)}) collective-permute-start(s32[1,1,1]{1,2,0:T(1,128)} %get-tuple-element.89), channel_id=1, source_target_pairs={{1,0},{2,1},{3,2},{0,3},{5,4},{6,5},{7,6},{4,7},{9,8},{10,9},{11,1... | collective-permute-start | bytes 20 | tf_op jit(solution)/shard_map/ppermute | solution.py:30
  199.5 4.8 %copy-start = (f32[4,128,128]{2,1,0:T(8,128)S(1)}, f32[4,128,128]{2,1,0:T(8,128)}, u32[]{:S(2)}) copy-start(f32[4,128,128]{2,1,0:T(8,128)} %param.5) | copy-start | bytes 786436
  199.5 4.8 %copy-start.1 = (s32[128,128]{1,0:T(8,128)S(1)}, s32[128,128]{1,0:T(8,128)}, u32[]{:S(2)}) copy-start(s32[128,128]{1,0:T(8,128)} %param.6) | copy-start | bytes 196612
  199.5 23.7 %all-to-all-start.1 = ((f32[64,4,4,2,128]{4,2,3,1,0:T(4,128)}), f32[64,4,4,2,128]{4,2,3,1,0:T(4,128)S(1)}, u32[]{:S(2)}, u32[]{:S(2)}) async-start(f32[64,4,4,2,128]{4,2,3,1,0:T(4,128)} %copy.19), calls=%async_computation.1 | async-start | bytes 2097152 | tf_op jit(solution)/shard_map/all_to_all | solution.py:153
  227.1 32.0 %collective-permute-start.2 = (f32[5,4,128,2]{2,1,3,0:T(4,128)S(1)}, f32[5,4,128,2]{2,1,3,0:T(4,128)S(1)}, u32[]{:S(2)}, u32[]{:S(2)}) collective-permute-start(f32[5,4,128,2]{2,1,3,0:T(4,128)S(1)} %copy.21), channel_id=1, source_target_pairs={{0,1},{1,2},{2,3},{3,0},{4,5},{5,6},{6,7},{7,4},{8,9},{9,10},{10,1... | collective-permute-start | bytes 61448 | tf_op jit(solution)/shard_map/ppermute | solution.py:29
  258.6 3.4 %collective-permute-start.3 = (f32[5,4,128,2]{2,1,3,0:T(4,128)S(1)}, f32[5,4,128,2]{2,1,3,0:T(4,128)S(1)}, u32[]{:S(2)}, u32[]{:S(2)}) collective-permute-start(f32[5,4,128,2]{2,1,3,0:T(4,128)S(1)} %copy.22), channel_id=1, source_target_pairs={{1,0},{2,1},{3,2},{0,3},{5,4},{6,5},{7,6},{4,7},{9,8},{10,9},{11,1... | collective-permute-start | bytes 61448 | tf_op jit(solution)/shard_map/ppermute | solution.py:30
  273.1 1.2 collective-permute-start.4
  273.6 3.5 %collective-permute-start.5 = (f32[5,4,128,2]{2,1,3,0:T(4,128)S(1)}, f32[5,4,128,2]{2,1,3,0:T(4,128)S(1)}, u32[]{:S(2)}, u32[]{:S(2)}) collective-permute-start(f32[5,4,128,2]{2,1,3,0:T(4,128)S(1)} %copy.26), channel_id=1, source_target_pairs={{1,0},{2,1},{3,2},{0,3},{5,4},{6,5},{7,6},{4,7},{9,8},{10,9},{11,1... | collective-permute-start | bytes 61448 | tf_op jit(solution)/shard_map/ppermute | solution.py:30
  288.2 1.3 collective-permute-start.6
  288.6 3.5 %collective-permute-start.7 = (f32[5,4,128,2]{2,1,3,0:T(4,128)S(1)}, f32[5,4,128,2]{2,1,3,0:T(4,128)S(1)}, u32[]{:S(2)}, u32[]{:S(2)}) collective-permute-start(f32[5,4,128,2]{2,1,3,0:T(4,128)S(1)} %copy.30), channel_id=1, source_target_pairs={{1,0},{2,1},{3,2},{0,3},{5,4},{6,5},{7,6},{4,7},{9,8},{10,9},{11,1... | collective-permute-start | bytes 61448 | tf_op jit(solution)/shard_map/ppermute | solution.py:30
where the time goes:
time: 301 us
  blocking collectives  159 us (53%)
  starting transfers between devices  54.3 us (18%)
  waiting for transfers between devices  29.6 us (10%)
  local copies, waits for them, and re-layouts  26.5 us (9%)
  other arithmetic  20.5 us (7%)
  matrix products  10.6 us (4%)
    all_gather x1, blocking collectives, on_device(): everyone = lax.all_gather(rimmed, 'dom', axis=0, tiled=True)  159 us
    ppermute x4, starting transfers between devices, padded_2(): before = lax.ppermute(last, axis, up)  32.5 us
    all_to_all x1, waiting for transfers between devices, on_device(): lax.all_to_all(mixed, 'dom', split_axis=0, concat_axis=3, tiled=True)  18.9 us
    all_to_all x1, starting transfers between devices, on_device(): lax.all_to_all(state, 'dom', split_axis=3, concat_axis=0, tiled=True)  15.2 us
    dot_general x1, matrix products, blend_members(): jnp.einsum('osx,sfkrx->ofkrx', mixing, block, precision=lax.Precision.HIG...  10.6 us
    ppermute x4, waiting for transfers between devices, padded_2(): after = lax.ppermute(initial, axis, down)  9.7 us
    slice x6, local copies, waits for them, and re-layouts, padded_2(): last = lax.slice_in_dim(x, length - width, length, axis=dim)  8.83 us
    concatenate x4, other arithmetic, padded_2(): x = jnp.concatenate([before, x, after], axis=dim)  8.49 us
  transfers between devices with their start and end apart: 10, of which 7 were waited for; matrix products, arithmetic and copies ran while one was open for 2% of the time, Pallas kernels for 0%

commit v1 on v0

v1 whole, which is shorter than its diff:
```python
import jax
import jax.numpy as jnp
from jax import lax
from jax.experimental import pallas as pl
from jax.experimental.pallas import tpu as pltpu
from jax.sharding import PartitionSpec as P

LEV = 4
FIELDS = 4
TILE = 64
BLEND = 8
STEPS = 3
LAT = 128
WIDTH = 128
HALO = 2 * STEPS
GROUPS = FIELDS * LEV + LEV
PAD = 8
ROWS = 32

time_step = 0.3
gravity = 1.0
drag_rate = 0.05
diffusion = 0.1
vertical_mix = 0.2
coriolis_base = 0.1
coriolis_slope = 0.3

VMEM_LIMIT = 16 * 1024 * 1024


def lanes_of(rows):
    return lax.broadcasted_iota(jnp.int32, (rows, WIDTH), 1)


def vmem(count):
    return [pl.BlockSpec(memory_space=pltpu.VMEM)] * count


def blend_kernel(table_ref, block_ref, out_ref):
    particles, rows, _ = block_ref.shape
    lane = lanes_of(8)
    position = lane % TILE
    near_left = position < BLEND
    near_right = position >= TILE - BLEND
    distance = jnp.where(near_left, position, TILE - 1 - position).astype(jnp.float32)
    weight = jnp.where(near_left | near_right, 0.5 + (distance + 0.5) / (2.0 * BLEND), 1.0)
    rest = 1.0 - weight
    first = lane < TILE
    zero = jnp.zeros_like(weight)
    weights = (
        jnp.where(first & near_left, rest, zero),
        jnp.where(first, weight, jnp.where(near_left, rest, zero)),
        jnp.where(first, jnp.where(near_right, rest, zero), weight),
        jnp.where(first, zero, jnp.where(near_right, rest, zero)),
    )

    def one(particle, carry):
        picks = [table_ref[tile, particle] for tile in range(4)]
        for row in range(0, rows, 8):
            parts = [block_ref[pick, row : row + 8, :] * w for pick, w in zip(picks, weights)]
            out_ref[particle, row : row + 8, :] = (parts[1] + parts[2]) + (parts[0] + parts[3])
        return carry

    lax.fori_loop(0, particles, one, 0, unroll=4)


def blend(table, block):
    return pl.pallas_call(
        blend_kernel,
        out_shape=jax.ShapeDtypeStruct(block.shape, block.dtype),
        in_specs=[pl.BlockSpec(memory_space=pltpu.SMEM)] + vmem(1),
        out_specs=pl.BlockSpec(memory_space=pltpu.VMEM),
        compiler_params=pltpu.CompilerParams(vmem_limit_bytes=VMEM_LIMIT),
        cost_estimate=pl.CostEstimate(flops=4 * block.size, bytes_accessed=8 * block.size, transcendentals=0),
        name="blend",
    )(table, block)


def masked_thickness(depth_ref, levels_ref, level, start, rows):
    wet = levels_ref[pl.ds(start, rows), :] > level
    return jnp.where(wet, depth_ref[level, pl.ds(start, rows), :], 0.0)


def pack_kernel(fields_ref, depth_ref, levels_ref, right_ref, left_ref):
    lane = lanes_of(8)
    slot_right = lane // HALO
    slot_left = ((lane + WIDTH - HALO) % WIDTH) // HALO

    def one(block, carry):
        start = pl.multiple_of(block * 8, 8)
        right = jnp.zeros((8, WIDTH), jnp.float32)
        left = jnp.zeros((8, WIDTH), jnp.float32)
        for group in range(GROUPS):
            if group < FIELDS * LEV:
                values = fields_ref[group, pl.ds(start, 8), :]
            else:
                values = masked_thickness(depth_ref, levels_ref, group - FIELDS * LEV, start, 8)
            turned = pltpu.roll(values, (HALO * group + HALO) % WIDTH, 1)
            right = jnp.where(slot_right == group, turned, right)
            left = jnp.where(slot_left == group, turned, left)
        right_ref[pl.ds(start, 8), :] = right
        left_ref[pl.ds(start, 8), :] = left
        return carry

    lax.fori_loop(0, LAT // 8, one, 0, unroll=4)


def pack(fields, depth, levels):
    shape = jax.ShapeDtypeStruct((LAT, WIDTH), jnp.float32)
    return pl.pallas_call(
        pack_kernel,
        out_shape=(shape, shape),
        in_specs=vmem(3),
        out_specs=tuple(vmem(2)),
        compiler_params=pltpu.CompilerParams(vmem_limit_bytes=VMEM_LIMIT),
        cost_estimate=pl.CostEstimate(flops=4 * fields.size, bytes_accessed=5 * fields.size, transcendentals=0),
        name="pack",
    )(fields, depth, levels)


def forecast_kernel(
    fields_ref, depth_ref, levels_ref, before_ref, after_ref, out_ref,
    height, zonal, merid, tracer, thick, height_part, flux, south, north,
):
    lane = lanes_of(ROWS)
    at_first = lane == 0
    at_last = lane == WIDTH - 1

    def east(pair):
        main, rim = (pltpu.roll(x, WIDTH - 1, 1) for x in pair)
        return jnp.where(at_last, rim, main), jnp.where(at_last, main, rim)

    def west(pair):
        main, rim = (pltpu.roll(x, 1, 1) for x in pair)
        return jnp.where(at_first, rim, main), jnp.where(at_first, main, rim)

    def slope(pair):
        return tuple(e - w for e, w in zip(east(pair), west(pair)))

    def rows_at(ref, side, level, start, shift):
        return ref[side, level, pl.ds(start + PAD + shift, ROWS), :]

    def blocks(body):
        def one(block, carry):
            body(pl.multiple_of(block * ROWS, ROWS))
            return carry

        lax.fori_loop(0, LAT // ROWS, one, 0)

    def put(ref, side, level, start, values):
        ref[side, level, pl.ds(pl.multiple_of(start + PAD, 8), ROWS), :] = values

    edge = jnp.zeros((PAD, WIDTH), jnp.float32)
    for ref in (height, flux, south, north):
        for side in range(2):
            for level in range(LEV):
                ref[side, level, 0:PAD, :] = edge
                ref[side, level, PAD + LAT : 2 * PAD + LAT, :] = edge

    sources = (height, zonal, merid, tracer)
    from_before = (lane // HALO) % 2 == 0

    def load(start):
        before = before_ref[pl.ds(start, ROWS), :]
        after = after_ref[pl.ds(start, ROWS), :]
        even = jnp.where(from_before, before, after)
        odd = jnp.where(from_before, after, before)
        for group in range(GROUPS):
            rim = pltpu.roll((even, odd)[group % 2], (2 * WIDTH - HALO - HALO * group) % WIDTH, 1)
            field, level = divmod(group, LEV)
            if field < FIELDS:
                put(sources[field], 0, level, start, fields_ref[group, pl.ds(start, ROWS), :])
                put(sources[field], 1, level, start, rim)
            else:
                put(thick, 0, level, start, masked_thickness(depth_ref, levels_ref, level, start, ROWS))
                put(thick, 1, level, start, rim)

    blocks(load)

    half = 0.5 * time_step
    keep = 1.0 - time_step * drag_rate

    for step in range(STEPS):
        last = step == STEPS - 1

        def winds(start):
            row = lax.broadcasted_iota(jnp.int32, (ROWS, WIDTH), 0) + start
            turn = time_step * (coriolis_base + coriolis_slope * row.astype(jnp.float32) / LAT)
            for level in range(LEV):
                h, u, v, c, t = (
                    [rows_at(ref, side, level, start, 0) for side in range(2)]
                    for ref in (height, zonal, merid, tracer, thick)
                )
                dh = slope(h)
                new_u, new_v, across, down, up = [], [], [], [], []
                for side in range(2):
                    dy = rows_at(height, side, level, start, 1) - rows_at(height, side, level, start, -1)
                    wet = t[side] > 0.0
                    one_u = keep * u[side] + turn * v[side] - (half * gravity) * dh[side]
                    one_v = keep * v[side] - turn * u[side] - (half * gravity) * dy
                    one_u = jnp.where(wet, one_u, 0.0)
                    one_v = jnp.where(wet, one_v, 0.0)
                    some, more = diffusion * c[side], half * c[side]
                    along, cross = more * one_u, more * one_v
                    new_u.append(one_u)
                    new_v.append(one_v)
                    across.append(t[side] * one_u)
                    down.append(some - along)
                    up.append(some + along)
                    put(flux, side, level, start, t[side] * one_v)
                    put(south, side, level, start, some - cross)
                    put(north, side, level, start, some + cross)
                du = slope(across)
                from_east, from_west = east(down), west(up)
                for side in range(2):
                    if last and side:
                        continue
                    if last:
                        out_ref[LEV + level, pl.ds(start, ROWS), :] = new_u[0]
                        out_ref[2 * LEV + level, pl.ds(start, ROWS), :] = new_v[0]
                    else:
                        put(zonal, side, level, start, new_u[side])
                        put(merid, side, level, start, new_v[side])
                    put(height_part, side, level, start, h[side] - half * du[side])
                    put(
                        tracer, side, level, start,
                        (1.0 - 4.0 * diffusion) * c[side] + (from_east[side] + from_west[side]),
                    )

        def levels(start):
            for side in range(1 if last else 2):
                wets = [rows_at(thick, side, level, start, 0) > 0.0 for level in range(LEV)]
                moved = []
                for level in range(LEV):
                    dy = rows_at(flux, side, level, start, 1) - rows_at(flux, side, level, start, -1)
                    new_h = rows_at(height_part, side, level, start, 0) - half * dy
                    new_h = jnp.where(wets[level], new_h, 0.0)
                    if last:
                        out_ref[level, pl.ds(start, ROWS), :] = new_h
                    else:
                        put(height, side, level, start, new_h)
                    new_c = rows_at(tracer, side, level, start, 0) + (
                        rows_at(south, side, level, start, 1) + rows_at(north, side, level, start, -1)
                    )
                    moved.append(jnp.where(wets[level], new_c, 0.0))
                swaps = [
                    jnp.where(wets[level] & wets[level + 1], vertical_mix * (moved[level + 1] - moved[level]), 0.0)
                    for level in range(LEV - 1)
                ]
                for level in range(LEV):
                    new_c = moved[level]
                    if level < LEV - 1:
                        new_c = new_c + swaps[level]
                    if level > 0:
                        new_c = new_c - swaps[level - 1]
                    if last:
                        out_ref[3 * LEV + level, pl.ds(start, ROWS), :] = new_c
                    else:
                        put(tracer, side, level, start, new_c)

        blocks(winds)
        blocks(levels)


def run_forecast(fields, depth, levels, before, after):
    scratch = pltpu.VMEM((2, LEV, LAT + 2 * PAD, WIDTH), jnp.float32)
    return pl.pallas_call(
        forecast_kernel,
        out_shape=jax.ShapeDtypeStruct(fields.shape, fields.dtype),
        in_specs=vmem(5),
        out_specs=pl.BlockSpec(memory_space=pltpu.VMEM),
        scratch_shapes=[scratch] * 9,
        compiler_params=pltpu.CompilerParams(vmem_limit_bytes=VMEM_LIMIT),
        cost_estimate=pl.CostEstimate(flops=150 * fields.size, bytes_accessed=12 * fields.size, transcendentals=0),
        name="forecast",
    )(fields, depth, levels, before, after)


def ring(values, axis, shift):
    size = lax.axis_size(axis)
    return lax.ppermute(values, axis, [(i, (i + shift) % size) for i in range(size)])


def tile_table(ancestors):
    own = ancestors[0, :, 0]
    left = ring(own[1:], "lon", 1)
    right = ring(own[:1], "lon", -1)
    mine = jnp.concatenate([left, own, right])
    size = lax.axis_size("dom")
    here = jnp.arange(size) == lax.axis_index("dom")
    table = jnp.where(here[None, :], mine[:, None], 0)
    bit = 1
    while bit < size:
        table = table + lax.ppermute(table, "dom", [(i, i ^ bit) for i in range(size)])
        bit *= 2
    return table


def on_device(state, level_thickness, wet_levels, ancestors):
    size = lax.axis_size("dom")
    table = tile_table(ancestors)
    chunks = state.reshape(size, -1, WIDTH)
    block = lax.all_to_all(chunks, "dom", split_axis=0, concat_axis=0, tiled=True)
    mixed = blend(table, block)
    back = lax.all_to_all(mixed, "dom", split_axis=0, concat_axis=0, tiled=True)
    fields = back.reshape(FIELDS * LEV, LAT, WIDTH)
    right, left = pack(fields, level_thickness, wet_levels)
    before = ring(right, "lon", 1)
    after = ring(left, "lon", -1)
    result = run_forecast(fields, level_thickness, wet_levels, before, after)
    return result.reshape(state.shape)


def solution(mesh):
    return jax.shard_map(
        on_device,
        mesh=mesh,
        in_specs=(
            P("dom", None, None, None, "lon"),
            P(None, None, "lon"),
            P(None, "lon"),
            P("dom", "lon", None),
        ),
        out_specs=P("dom", None, None, None, "lon"),
        check_vma=False,
    )
```

time: 301 us -> 115 us (0.38)
  blocking collectives: 159 us -> 33.3 us
  local copies, waits for them, and re-layouts: 26.5 us -> 0.6 us
  other arithmetic: 20.5 us -> 1.54 us
  starting transfers between devices: 54.3 us -> 41.3 us
  matrix products: 10.6 us -> 0 us
  Pallas kernels: 0 us -> 9.19 us
    all_gather x1 -> x0, blocking collectives: 159 us -> none  [on_device(): everyone = lax.all_gather(rimmed, 'dom', axis=0, tiled=True)]
    all_to_all x0 -> x1, blocking collectives: none -> 33.3 us  [on_device(): back = lax.all_to_all(mixed, 'dom', split_axis=0, concat_axis=0, tiled=True)]
    all_to_all x2 -> x1, waiting for transfers between devices: 18.9 us -> 0.01 us  [on_device(): lax.all_to_all(chunks, 'dom', split_axis=0, concat_axis=0, tiled=True)]
    ppermute x8 -> x10, waiting for transfers between devices: 10.7 us -> 28.8 us  [the longest x6 21.7 us: tile_table(): lax.ppermute(table, 'dom', [(i, i ^ bit) for i in range(size)])]
    dot_general x1 -> x0, matrix products: 10.6 us -> none  [blend_members(): jnp.einsum('osx,sfkrx->ofkrx', mixing, block, precision=lax.Precision.HIG...]
    slice x22 -> x1, local copies, waits for them, and re-layouts: 11.1 us -> 0.58 us  [tile_table(): left = ring(own[1:], 'lon', 1)]
    pallas_call x0 -> x3, Pallas kernels: none -> 9.19 us  [the longest x1 7.51 us: run_forecast(): pl.pallas_call(forecast_kernel, out_shape=jax.ShapeDtypeStruct(fields.sha...]
    concatenate x7 -> x1, other arithmetic: 10.1 us -> 1.3 us  [tile_table(): mine = jnp.concatenate([left, own, right])]
  transfers between devices with their start and end apart: 10 -> 11, of which waited for: 7 -> 10; matrix products, arithmetic and copies ran while one was open for 2% -> 2% of each run, Pallas kernels for 0% -> 0%
where the time goes in v1:
time: 115 us
  starting transfers between devices  41.3 us (36%)
  blocking collectives  33.3 us (29%)
  waiting for transfers between devices  28.8 us (25%)
  Pallas kernels  9.19 us (8%)
  other arithmetic  1.54 us (1%)
    all_to_all x1, blocking collectives, on_device(): back = lax.all_to_all(mixed, 'dom', split_axis=0, concat_axis=0, tiled=True)  33.3 us
    ppermute x6, waiting for transfers between devices, tile_table(): lax.ppermute(table, 'dom', [(i, i ^ bit) for i in range(size)])  21.7 us
    all_to_all x1, starting transfers between devices, on_device(): lax.all_to_all(chunks, 'dom', split_axis=0, concat_axis=0, tiled=True)  15.2 us
    ppermute x6, starting transfers between devices, tile_table(): lax.ppermute(table, 'dom', [(i, i ^ bit) for i in range(size)])  14.7 us
    ppermute x4, starting transfers between devices, ring(): lax.ppermute(values, axis, [(i, (i + shift) % size) for i in range(size)])  11.3 us
    pallas_call x1, Pallas kernels, run_forecast(): pl.pallas_call(forecast_kernel, out_shape=jax.ShapeDtypeStruct(fields.sha...  7.51 us
    ppermute x4, waiting for transfers between devices, ring(): lax.ppermute(values, axis, [(i, (i + shift) % size) for i in range(size)])  7.15 us
  transfers between devices with their start and end apart: 11, of which 10 were waited for; matrix products, arithmetic and copies ran while one was open for 2% of the time, Pallas kernels for 0%

profile of v1, /device:TPU:1, one launch (start us, length us, event | category | flops | bytes accessed | tf_op | source)
XLA Modules:
  0.0 114.8 jit_solution(115535869046546768)
XLA Ops:
  0.0 15.2 %all-to-all-start = ((f32[64,32,128]{2,1,0:T(8,128)}), f32[64,32,128]{2,1,0:T(8,128)S(1)}, u32[]{:S(2)}, u32[]{:S(2)}) async-start(f32[64,32,128]{2,1,0:T(8,128)} %bitcast.8), calls=%async_computation | async-start | bytes 2097152 | tf_op jit(solution)/shard_map/all_to_all | solution.py:303
  15.3 0.6 fusion.1
  15.9 1.2 %collective-permute-start = (s32[1]{0:T(128)}, s32[1]{0:T(128)}, u32[]{:S(2)}, u32[]{:S(2)}) collective-permute-start(s32[1]{0:T(128)} %bitcast), channel_id=1, source_target_pairs={{0,1},{1,2},{2,3},{3,0},{4,5},{5,6},{6,7},{7,4},{8,9},{9,10},{10,1... | collective-permute-start | bytes 20 | tf_op jit(solution)/shard_map/ppermute | solution.py:281
  17.1 0.0 collective-permute-start.1
  17.1 0.8 collective-permute-done
  17.9 2.6 %collective-permute-done.1 = s32[1]{0:T(128)} collective-permute-done((s32[1]{0:T(128)}, s32[1]{0:T(128)}, u32[]{:S(2)}, u32[]{:S(2)}) %collective-permute-start.1) | collective-permute-done | bytes 36 | tf_op jit(solution)/shard_map/ppermute | solution.py:281
  20.6 1.3 %pad_add_fusion = s32[4]{0:T(128)S(1)} fusion(s32[1]{0:T(128)} %collective-permute-done.1, s32[2]{0:T(128)S(1)} %bitcast.9, s32[1]{0:T(128)} %collective-permute-done), kind=kLoop, calls=%fused_computation.1 | loop fusion | flops 8 | bytes 32 | tf_op jit(solution)/shard_map/concatenate | solution.py:288
  21.9 0.1 broadcast_select_fusion
  21.9 1.3 %collective-permute-start.2 = (s32[4,64]{1,0:T(4,128)S(1)}, s32[4,64]{1,0:T(4,128)S(1)}, u32[]{:S(2)}, u32[]{:S(2)}) collective-permute-start(s32[4,64]{1,0:T(4,128)S(1)} %broadcast_select_fusion), channel_id=1, source_target_pairs={{0,4},{4,0},{8,12},{12,8},{16,20},{20,16},{24,28},{28,24},{32,36},... | collective-permute-start | bytes 3080 | tf_op jit(solution)/shard_map/ppermute | solution.py:294
  23.2 14.5 %collective-permute-done.2 = s32[4,64]{1,0:T(4,128)S(1)} collective-permute-done((s32[4,64]{1,0:T(4,128)S(1)}, s32[4,64]{1,0:T(4,128)S(1)}, u32[]{:S(2)}, u32[]{:S(2)}) %collective-permute-start.2) | collective-permute-done | bytes 1056 | tf_op jit(solution)/shard_map/ppermute | solution.py:294
  37.8 0.1 fusion
  37.8 1.6 %collective-permute-start.3 = (s32[4,64]{1,0:T(4,128)S(1)}, s32[4,64]{1,0:T(4,128)S(1)}, u32[]{:S(2)}, u32[]{:S(2)}) collective-permute-start(s32[4,64]{1,0:T(4,128)S(1)} %fusion), channel_id=1, source_target_pairs={{0,8},{4,12},{8,0},{12,4},{16,24},{20,28},{24,16},{28,20},{32,40},... | collective-permute-start | bytes 3080 | tf_op jit(solution)/shard_map/ppermute | solution.py:294
  39.4 2.0 %collective-permute-done.3 = s32[4,64]{1,0:T(4,128)S(1)} collective-permute-done((s32[4,64]{1,0:T(4,128)S(1)}, s32[4,64]{1,0:T(4,128)S(1)}, u32[]{:S(2)}, u32[]{:S(2)}) %collective-permute-start.3) | collective-permute-done | bytes 1056 | tf_op jit(solution)/shard_map/ppermute | solution.py:294
  41.5 0.1 fusion.2
  41.5 5.2 %collective-permute-start.4 = (s32[4,64]{1,0:T(4,128)S(1)}, s32[4,64]{1,0:T(4,128)S(1)}, u32[]{:S(2)}, u32[]{:S(2)}) collective-permute-start(s32[4,64]{1,0:T(4,128)S(1)} %fusion.2), channel_id=1, source_target_pairs={{0,16},{4,20},{8,24},{12,28},{16,0},{20,4},{24,8},{28,12},{32,48},... | collective-permute-start | bytes 3080 | tf_op jit(solution)/shard_map/ppermute | solution.py:294
  46.7 1.2 %collective-permute-done.4 = s32[4,64]{1,0:T(4,128)S(1)} collective-permute-done((s32[4,64]{1,0:T(4,128)S(1)}, s32[4,64]{1,0:T(4,128)S(1)}, u32[]{:S(2)}, u32[]{:S(2)}) %collective-permute-start.4) | collective-permute-done | bytes 1056 | tf_op jit(solution)/shard_map/ppermute | solution.py:294
  47.9 1.2 %collective-permute-start.5 = (s32[4,64]{1,0:T(4,128)S(1)}, s32[4,64]{1,0:T(4,128)S(1)}, u32[]{:S(2)}, u32[]{:S(2)}) collective-permute-start(s32[4,64]{1,0:T(4,128)S(1)} %add.20), channel_id=1, source_target_pairs={{0,32},{4,36},{8,40},{12,44},{16,48},{20,52},{24,56},{28,60},{32,0... | collective-permute-start | bytes 3080 | tf_op jit(solution)/shard_map/ppermute | solution.py:294
  49.1 1.5 %collective-permute-done.5 = s32[4,64]{1,0:T(4,128)S(1)} collective-permute-done((s32[4,64]{1,0:T(4,128)S(1)}, s32[4,64]{1,0:T(4,128)S(1)}, u32[]{:S(2)}, u32[]{:S(2)}) %collective-permute-start.5) | collective-permute-done | bytes 1056 | tf_op jit(solution)/shard_map/ppermute | solution.py:294
  50.6 2.7 %collective-permute-start.6 = (s32[4,64]{1,0:T(4,128)S(1)}, s32[4,64]{1,0:T(4,128)S(1)}, u32[]{:S(2)}, u32[]{:S(2)}) collective-permute-start(s32[4,64]{1,0:T(4,128)S(1)} %add.21), channel_id=1, source_target_pairs={{0,64},{4,68},{8,72},{12,76},{16,80},{20,84},{24,88},{28,92},{32,9... | collective-permute-start | bytes 3080 | tf_op jit(solution)/shard_map/ppermute | solution.py:294
  53.3 1.2 %collective-permute-done.6 = s32[4,64]{1,0:T(4,128)S(1)} collective-permute-done((s32[4,64]{1,0:T(4,128)S(1)}, s32[4,64]{1,0:T(4,128)S(1)}, u32[]{:S(2)}, u32[]{:S(2)}) %collective-permute-start.6) | collective-permute-done | bytes 1056 | tf_op jit(solution)/shard_map/ppermute | solution.py:294
  54.6 2.8 %collective-permute-start.7 = (s32[4,64]{1,0:T(4,128)S(1)}, s32[4,64]{1,0:T(4,128)S(1)}, u32[]{:S(2)}, u32[]{:S(2)}) collective-permute-start(s32[4,64]{1,0:T(4,128)S(1)} %add.22), channel_id=1, source_target_pairs={{0,128},{4,132},{8,136},{12,140},{16,144},{20,148},{24,152},{28,15... | collective-permute-start | bytes 3080 | tf_op jit(solution)/shard_map/ppermute | solution.py:294
  57.3 1.2 %collective-permute-done.7 = s32[4,64]{1,0:T(4,128)S(1)} collective-permute-done((s32[4,64]{1,0:T(4,128)S(1)}, s32[4,64]{1,0:T(4,128)S(1)}, u32[]{:S(2)}, u32[]{:S(2)}) %collective-permute-start.7) | collective-permute-done | bytes 1056 | tf_op jit(solution)/shard_map/ppermute | solution.py:294
  58.5 1.1 blend.1
  59.6 0.0 copy-start
  59.6 0.0 copy-start.1
  59.6 33.3 %all_to_all.10 = f32[64,32,128]{2,1,0:T(8,128)S(1)} all-to-all(f32[64,32,128]{2,1,0:T(8,128)S(1)} %blend.1), channel_id=1, replica_groups=mesh['dom'=64,'lon'=4] {'dom'}, dimensions={0} | all-to-all | bytes 2097152 | tf_op jit(solution)/shard_map/all_to_all | solution.py:305
  92.9 0.6 pack.1
  93.5 10.1 %collective-permute-start.8 = (f32[128,128]{1,0:T(8,128)S(1)}, f32[128,128]{1,0:T(8,128)S(1)}, u32[]{:S(2)}, u32[]{:S(2)}) collective-permute-start(f32[128,128]{1,0:T(8,128)S(1)} %get-tuple-element.7), channel_id=1, source_target_pairs={{0,1},{1,2},{2,3},{3,0},{4,5},{5,6},{6,7},{7,4},{8,9},{9,10},{10,1... | collective-permute-start | bytes 196616 | tf_op jit(solution)/shard_map/ppermute | solution.py:281
  103.6 0.0 collective-permute-start.9
  103.6 1.3 %collective-permute-done.8.before_ref = f32[128,128]{1,0:T(8,128)S(1)} collective-permute-done((f32[128,128]{1,0:T(8,128)S(1)}, f32[128,128]{1,0:T(8,128)S(1)}, u32[]{:S(2)}, u32[]{:S(2)}) %collective-permute-start.8) | collective-permute-done | bytes 65568 | tf_op jit(solution)/shard_map/ppermute | solution.py:281
  105.0 2.4 %collective-permute-done.9.after_ref = f32[128,128]{1,0:T(8,128)S(1)} collective-permute-done((f32[128,128]{1,0:T(8,128)S(1)}, f32[128,128]{1,0:T(8,128)S(1)}, u32[]{:S(2)}, u32[]{:S(2)}) %collective-permute-start.9) | collective-permute-done | bytes 65568 | tf_op jit(solution)/shard_map/ppermute | solution.py:281
  107.3 7.5 %forecast.1 = f32[16,128,128]{2,1,0:T(8,128)} custom-call(f32[16,128,128]{2,1,0:T(8,128)S(1)} %bitcast.7, f32[4,128,128]{2,1,0:T(8,128)S(1)} %copy-done, s32[128,128]{1,0:T(8,128)S(1)} %copy-done.1, f32[128,128]{1,0:T(8,128)S(1)} %collective-permute-done.8.before_ref, f32[128,128]{1,0:T(8,128)S(1)} %collective-permute-done.9.after_ref), custom_call_target="tpu_custom_call" | custom-call | flops 39321600 | bytes 3145728 | tf_op jit(solution)/shard_map/forecast/pallas_call | solution.py:267
  (10 shorter events, 0.0 us)
Async XLA Ops:
  0.0 15.3 %copy-start.2 = (s32[1,2,1]{1,2,0:T(1,128)S(1)}, s32[1,2,1]{1,2,0:T(1,128)}, u32[]{:S(2)}) copy-start(s32[1,2,1]{1,2,0:T(1,128)} %param.7) | copy-start | bytes 28
  0.0 58.5 %all-to-all-start = ((f32[64,32,128]{2,1,0:T(8,128)}), f32[64,32,128]{2,1,0:T(8,128)S(1)}, u32[]{:S(2)}, u32[]{:S(2)}) async-start(f32[64,32,128]{2,1,0:T(8,128)} %bitcast.8), calls=%async_computation | async-start | bytes 2097152 | tf_op jit(solution)/shard_map/all_to_all | solution.py:303
  15.9 2.1 %collective-permute-start = (s32[1]{0:T(128)}, s32[1]{0:T(128)}, u32[]{:S(2)}, u32[]{:S(2)}) collective-permute-start(s32[1]{0:T(128)} %bitcast), channel_id=1, source_target_pairs={{0,1},{1,2},{2,3},{3,0},{4,5},{5,6},{6,7},{7,4},{8,9},{9,10},{10,1... | collective-permute-start | bytes 20 | tf_op jit(solution)/shard_map/ppermute | solution.py:281
  17.1 3.5 %collective-permute-start.1 = (s32[1]{0:T(128)}, s32[1]{0:T(128)}, u32[]{:S(2)}, u32[]{:S(2)}) collective-permute-start(s32[1]{0:T(128)} %bitcast.2), channel_id=1, source_target_pairs={{0,3},{1,0},{2,1},{3,2},{4,7},{5,4},{6,5},{7,6},{8,11},{9,8},{10,9... | collective-permute-start | bytes 20 | tf_op jit(solution)/shard_map/ppermute | solution.py:281
  21.9 15.8 %collective-permute-start.2 = (s32[4,64]{1,0:T(4,128)S(1)}, s32[4,64]{1,0:T(4,128)S(1)}, u32[]{:S(2)}, u32[]{:S(2)}) collective-permute-start(s32[4,64]{1,0:T(4,128)S(1)} %broadcast_select_fusion), channel_id=1, source_target_pairs={{0,4},{4,0},{8,12},{12,8},{16,20},{20,16},{24,28},{28,24},{32,36},... | collective-permute-start | bytes 3080 | tf_op jit(solution)/shard_map/ppermute | solution.py:294
  37.8 3.6 %collective-permute-start.3 = (s32[4,64]{1,0:T(4,128)S(1)}, s32[4,64]{1,0:T(4,128)S(1)}, u32[]{:S(2)}, u32[]{:S(2)}) collective-permute-start(s32[4,64]{1,0:T(4,128)S(1)} %fusion), channel_id=1, source_target_pairs={{0,8},{4,12},{8,0},{12,4},{16,24},{20,28},{24,16},{28,20},{32,40},... | collective-permute-start | bytes 3080 | tf_op jit(solution)/shard_map/ppermute | solution.py:294
  41.5 6.3 %collective-permute-start.4 = (s32[4,64]{1,0:T(4,128)S(1)}, s32[4,64]{1,0:T(4,128)S(1)}, u32[]{:S(2)}, u32[]{:S(2)}) collective-permute-start(s32[4,64]{1,0:T(4,128)S(1)} %fusion.2), channel_id=1, source_target_pairs={{0,16},{4,20},{8,24},{12,28},{16,0},{20,4},{24,8},{28,12},{32,48},... | collective-permute-start | bytes 3080 | tf_op jit(solution)/shard_map/ppermute | solution.py:294
  47.9 2.7 %collective-permute-start.5 = (s32[4,64]{1,0:T(4,128)S(1)}, s32[4,64]{1,0:T(4,128)S(1)}, u32[]{:S(2)}, u32[]{:S(2)}) collective-permute-start(s32[4,64]{1,0:T(4,128)S(1)} %add.20), channel_id=1, source_target_pairs={{0,32},{4,36},{8,40},{12,44},{16,48},{20,52},{24,56},{28,60},{32,0... | collective-permute-start | bytes 3080 | tf_op jit(solution)/shard_map/ppermute | solution.py:294
  50.6 3.9 %collective-permute-start.6 = (s32[4,64]{1,0:T(4,128)S(1)}, s32[4,64]{1,0:T(4,128)S(1)}, u32[]{:S(2)}, u32[]{:S(2)}) collective-permute-start(s32[4,64]{1,0:T(4,128)S(1)} %add.21), channel_id=1, source_target_pairs={{0,64},{4,68},{8,72},{12,76},{16,80},{20,84},{24,88},{28,92},{32,9... | collective-permute-start | bytes 3080 | tf_op jit(solution)/shard_map/ppermute | solution.py:294
  54.6 3.9 %collective-permute-start.7 = (s32[4,64]{1,0:T(4,128)S(1)}, s32[4,64]{1,0:T(4,128)S(1)}, u32[]{:S(2)}, u32[]{:S(2)}) collective-permute-start(s32[4,64]{1,0:T(4,128)S(1)} %add.22), channel_id=1, source_target_pairs={{0,128},{4,132},{8,136},{12,140},{16,144},{20,148},{24,152},{28,15... | collective-permute-start | bytes 3080 | tf_op jit(solution)/shard_map/ppermute | solution.py:294
  59.6 33.3 %copy-start = (f32[4,128,128]{2,1,0:T(8,128)S(1)}, f32[4,128,128]{2,1,0:T(8,128)}, u32[]{:S(2)}) copy-start(f32[4,128,128]{2,1,0:T(8,128)} %depth_ref.3) | copy-start | bytes 786436
  59.6 33.3 %copy-start.1 = (s32[128,128]{1,0:T(8,128)S(1)}, s32[128,128]{1,0:T(8,128)}, u32[]{:S(2)}) copy-start(s32[128,128]{1,0:T(8,128)} %levels_ref.3) | copy-start | bytes 196612
  93.5 11.4 %collective-permute-start.8 = (f32[128,128]{1,0:T(8,128)S(1)}, f32[128,128]{1,0:T(8,128)S(1)}, u32[]{:S(2)}, u32[]{:S(2)}) collective-permute-start(f32[128,128]{1,0:T(8,128)S(1)} %get-tuple-element.7), channel_id=1, source_target_pairs={{0,1},{1,2},{2,3},{3,0},{4,5},{5,6},{6,7},{7,4},{8,9},{9,10},{10,1... | collective-permute-start | bytes 196616 | tf_op jit(solution)/shard_map/ppermute | solution.py:281
  103.6 3.7 %collective-permute-start.9 = (f32[128,128]{1,0:T(8,128)S(1)}, f32[128,128]{1,0:T(8,128)S(1)}, u32[]{:S(2)}, u32[]{:S(2)}) collective-permute-start(f32[128,128]{1,0:T(8,128)S(1)} %get-tuple-element.8), channel_id=1, source_target_pairs={{0,3},{1,0},{2,1},{3,2},{4,7},{5,4},{6,5},{7,6},{8,11},{9,8},{10,9... | collective-permute-start | bytes 196616 | tf_op jit(solution)/shard_map/ppermute | solution.py:281

commit v2 on v1

--- a/solution.py
+++ b/solution.py
@@ -15,7 +15,7 @@
 HALO = 2 * STEPS
 GROUPS = FIELDS * LEV + LEV
 PAD = 8
-ROWS = 32
+ROWS = 128
 
 time_step = 0.3
 gravity = 1.0
@@ -36,8 +36,39 @@
     return [pl.BlockSpec(memory_space=pltpu.VMEM)] * count
 
 
-def blend_kernel(table_ref, block_ref, out_ref):
-    particles, rows, _ = block_ref.shape
+def chunk_kernel(state_ref, own_ref, left_ref, right_ref, out_ref):
+    height = state_ref.shape[1]
+    lane = lanes_of(1)
+    picks = (left_ref[1], own_ref[0], own_ref[1], right_ref[0])
+    row = jnp.zeros((1, WIDTH), jnp.int32)
+    for tile, pick in enumerate(picks):
+        row = jnp.where(lane == tile, pick, row)
+    row = row.astype(jnp.float32)
+    for chunk in range(state_ref.shape[0]):
+        base = chunk * (height + 1)
+        out_ref[base : base + height, :] = state_ref[chunk]
+        out_ref[base + height : base + height + 1, :] = row
+
+
+def make_chunks(chunks, own, left, right):
+    count, height, width = chunks.shape
+    shape = (count * (height + 1), width)
+    return pl.pallas_call(
+        chunk_kernel,
+        out_shape=jax.ShapeDtypeStruct(shape, chunks.dtype),
+        in_specs=vmem(1) + [pl.BlockSpec(memory_space=pltpu.SMEM)] * 3,
+        out_specs=pl.BlockSpec(memory_space=pltpu.VMEM),
+        compiler_params=pltpu.CompilerParams(vmem_limit_bytes=VMEM_LIMIT),
+        cost_estimate=pl.CostEstimate(flops=0, bytes_accessed=8 * chunks.size, transcendentals=0),
+        name="chunks",
+    )(chunks, own, left, right)
+
+
+def blend_kernel(block_ref, out_ref, numbers_ref, table_ref, sem):
+    particles, rows, _ = out_ref.shape
+    numbers_ref[...] = block_ref[pl.ds(rows, particles, stride=rows + 1), :].astype(jnp.int32)
+    copy = pltpu.make_async_copy(numbers_ref, table_ref, sem)
+    copy.start()
     lane = lanes_of(8)
     position = lane % TILE
     near_left = position < BLEND
@@ -53,27 +84,35 @@
         jnp.where(first, jnp.where(near_right, rest, zero), weight),
         jnp.where(first, zero, jnp.where(near_right, rest, zero)),
     )
+    copy.wait()
 
     def one(particle, carry):
-        picks = [table_ref[tile, particle] for tile in range(4)]
+        picks = [table_ref[particle, tile] * (rows + 1) for tile in range(4)]
         for row in range(0, rows, 8):
-            parts = [block_ref[pick, row : row + 8, :] * w for pick, w in zip(picks, weights)]
+            parts = [block_ref[pl.ds(pick + row, 8), :] * w for pick, w in zip(picks, weights)]
             out_ref[particle, row : row + 8, :] = (parts[1] + parts[2]) + (parts[0] + parts[3])
         return carry
 
     lax.fori_loop(0, particles, one, 0, unroll=4)
 
 
-def blend(table, block):
+def blend(block, particles):
+    rows = block.shape[0] // particles - 1
+    shape = (particles, rows, WIDTH)
     return pl.pallas_call(
         blend_kernel,
-        out_shape=jax.ShapeDtypeStruct(block.shape, block.dtype),
-        in_specs=[pl.BlockSpec(memory_space=pltpu.SMEM)] + vmem(1),
+        out_shape=jax.ShapeDtypeStruct(shape, block.dtype),
+        in_specs=vmem(1),
         out_specs=pl.BlockSpec(memory_space=pltpu.VMEM),
+        scratch_shapes=[
+            pltpu.VMEM((particles, WIDTH), jnp.int32),
+            pltpu.SMEM((particles, WIDTH), jnp.int32),
+            pltpu.SemaphoreType.DMA,
+        ],
         compiler_params=pltpu.CompilerParams(vmem_limit_bytes=VMEM_LIMIT),
         cost_estimate=pl.CostEstimate(flops=4 * block.size, bytes_accessed=8 * block.size, transcendentals=0),
         name="blend",
-    )(table, block)
+    )(block)
 
 
 def masked_thickness(depth_ref, levels_ref, level, start, rows):
@@ -141,14 +180,11 @@
         return ref[side, level, pl.ds(start + PAD + shift, ROWS), :]
 
     def blocks(body):
-        def one(block, carry):
-            body(pl.multiple_of(block * ROWS, ROWS))
-            return carry
-
-        lax.fori_loop(0, LAT // ROWS, one, 0)
+        for block in range(LAT // ROWS):
+            body(block * ROWS)
 
     def put(ref, side, level, start, values):
-        ref[side, level, pl.ds(pl.multiple_of(start + PAD, 8), ROWS), :] = values
+        ref[side, level, pl.ds(start + PAD, ROWS), :] = values
 
     edge = jnp.zeros((PAD, WIDTH), jnp.float32)
     for ref in (height, flux, south, north):
@@ -207,9 +243,10 @@
                     across.append(t[side] * one_u)
                     down.append(some - along)
                     up.append(some + along)
-                    put(flux, side, level, start, t[side] * one_v)
-                    put(south, side, level, start, some - cross)
-                    put(north, side, level, start, some + cross)
+                    if not (last and side):
+                        put(flux, side, level, start, t[side] * one_v)
+                        put(south, side, level, start, some - cross)
+                        put(north, side, level, start, some + cross)
                 du = slope(across)
                 from_east, from_west = east(down), west(up)
                 for side in range(2):
@@ -281,27 +318,15 @@
     return lax.ppermute(values, axis, [(i, (i + shift) % size) for i in range(size)])
 
 
-def tile_table(ancestors):
-    own = ancestors[0, :, 0]
-    left = ring(own[1:], "lon", 1)
-    right = ring(own[:1], "lon", -1)
-    mine = jnp.concatenate([left, own, right])
-    size = lax.axis_size("dom")
-    here = jnp.arange(size) == lax.axis_index("dom")
-    table = jnp.where(here[None, :], mine[:, None], 0)
-    bit = 1
-    while bit < size:
-        table = table + lax.ppermute(table, "dom", [(i, i ^ bit) for i in range(size)])
-        bit *= 2
-    return table
-
-
 def on_device(state, level_thickness, wet_levels, ancestors):
     size = lax.axis_size("dom")
-    table = tile_table(ancestors)
-    chunks = state.reshape(size, -1, WIDTH)
-    block = lax.all_to_all(chunks, "dom", split_axis=0, concat_axis=0, tiled=True)
-    mixed = blend(table, block)
+    own = ancestors.reshape(-1)
+    left = ring(own, "lon", 1)
+    right = ring(own, "lon", -1)
+    chunks = make_chunks(state.reshape(size, -1, WIDTH), own, left, right)
+    sent = chunks.reshape(size, -1, 1, WIDTH)
+    block = lax.all_to_all(sent, "dom", split_axis=0, concat_axis=0, tiled=True)
+    mixed = blend(block.reshape(chunks.shape), size)
     back = lax.all_to_all(mixed, "dom", split_axis=0, concat_axis=0, tiled=True)
     fields = back.reshape(FIELDS * LEV, LAT, WIDTH)
     right, left = pack(fields, level_thickness, wet_levels)

time: 115 us -> 99.4 us (0.86)
  blocking collectives: 33.3 us -> 75.3 us
  starting transfers between devices: 41.3 us -> 8.92 us
  waiting for transfers between devices: 28.8 us -> 4.94 us
  other arithmetic: 1.54 us -> 0 us
  local copies, waits for them, and re-layouts: 0.6 us -> 1.89 us
    all_to_all x0 -> x1, blocking collectives: none -> 41.2 us  [on_device(): block = lax.all_to_all(sent, 'dom', split_axis=0, concat_axis=0, tiled=True)]
    ppermute x6 -> x0, waiting for transfers between devices: 21.7 us -> none  [tile_table(): lax.ppermute(table, 'dom', [(i, i ^ bit) for i in range(size)])]
    all_to_all x1 -> x0, starting transfers between devices: 15.2 us -> none  [on_device(): lax.all_to_all(chunks, 'dom', split_axis=0, concat_axis=0, tiled=True)]
    ppermute x6 -> x0, starting transfers between devices: 14.7 us -> none  [tile_table(): lax.ppermute(table, 'dom', [(i, i ^ bit) for i in range(size)])]
    ppermute x4, starting transfers between devices: 11.3 us -> 8.92 us  [ring(): lax.ppermute(values, axis, [(i, (i + shift) % size) for i in range(size)])]
    ppermute x4, waiting for transfers between devices: 7.15 us -> 4.94 us  [ring(): lax.ppermute(values, axis, [(i, (i + shift) % size) for i in range(size)])]
    pallas_call x1, Pallas kernels: 7.51 us -> 5.38 us  [run_forecast(): pl.pallas_call(forecast_kernel, out_shape=jax.ShapeDtypeStruct(fields.sha...]
    unnamed x6 -> x8, local copies, waits for them, and re-layouts: 0.02 us -> 1.89 us
  transfers between devices with their start and end apart: 11 -> 4, of which waited for: 10 -> 4; matrix products, arithmetic and copies ran while one was open for 2% -> 0% of each run, Pallas kernels for 0% -> 0%
where the time goes in v2:
time: 99.4 us; the launch traced here: 99.2 us
  blocking collectives  75.3 us (76%)
  starting transfers between devices  8.92 us (9%)
  Pallas kernels  8.12 us (8%)
  waiting for transfers between devices  4.94 us (5%)
  local copies, waits for them, and re-layouts  1.89 us (2%)
    all_to_all x1, blocking collectives, on_device(): block = lax.all_to_all(sent, 'dom', split_axis=0, concat_axis=0, tiled=True)  41.2 us
    all_to_all x1, blocking collectives, on_device(): back = lax.all_to_all(mixed, 'dom', split_axis=0, concat_axis=0, tiled=True)  34.1 us
    ppermute x4, starting transfers between devices, ring(): lax.ppermute(values, axis, [(i, (i + shift) % size) for i in range(size)])  8.92 us
    pallas_call x1, Pallas kernels, run_forecast(): pl.pallas_call(forecast_kernel, out_shape=jax.ShapeDtypeStruct(fields.sha...  5.38 us
    ppermute x4, waiting for transfers between devices, ring(): lax.ppermute(values, axis, [(i, (i + shift) % size) for i in range(size)])  4.94 us
  transfers between devices with their start and end apart: 4, of which 4 were waited for; matrix products, arithmetic and copies ran while one was open for 0% of the time, Pallas kernels for 0%

profile of v2, /device:TPU:1, one launch (start us, length us, event | category | flops | bytes accessed | tf_op | source)
XLA Modules:
  0.0 99.2 jit_solution(13985802821039062102)
XLA Ops:
  0.0 3.2 %collective-permute-start.1 = (s32[2]{0:T(128)}, s32[2]{0:T(128)S(1)}, u32[]{:S(2)}, u32[]{:S(2)}) collective-permute-start(s32[2]{0:T(128)} %bitcast.11), channel_id=1, source_target_pairs={{0,3},{1,0},{2,1},{3,2},{4,7},{5,4},{6,5},{7,6},{8,11},{9,8},{10,9... | collective-permute-start | bytes 32 | tf_op jit(solution)/shard_map/ppermute | solution.py:318
  3.2 0.0 collective-permute-start
  3.2 0.9 collective-permute-done.1.right_ref
  4.2 0.3 collective-permute-done.left_ref
  4.5 0.0 copy-start
  4.5 1.2 %copy-done = f32[1,4,4,128,128]{4,3,2,1,0:T(8,128)S(1)} copy-done((f32[1,4,4,128,128]{4,3,2,1,0:T(8,128)S(1)}, f32[1,4,4,128,128]{4,3,2,1,0:T(8,128)}, u32[]{:S(2)}) %copy-start) | copy-done | bytes 1048600
  5.7 0.0 copy-start.3
  5.7 0.7 copy-done.3
  6.4 0.6 chunks.1
  7.0 41.2 %all_to_all.10 = f32[64,33,1,128]{3,2,1,0:T(1,128)S(1)} all-to-all(f32[64,33,1,128]{3,2,1,0:T(1,128)S(1)} %bitcast.8), channel_id=1, replica_groups=mesh['dom'=64,'lon'=4] {'dom'}, dimensions={0} | all-to-all | bytes 2162688 | tf_op jit(solution)/shard_map/all_to_all | solution.py:328
  48.2 1.5 %blend.1 = f32[64,32,128]{2,1,0:T(8,128)S(1)} custom-call(f32[2112,128]{1,0:T(8,128)S(1)} %bitcast.9), custom_call_target="tpu_custom_call" | custom-call | flops 1081344 | bytes 2162688 | tf_op jit(solution)/shard_map/blend/pallas_call | solution.py:102
  49.7 0.0 copy-start.1
  49.7 0.0 copy-start.2
  49.8 34.1 %all_to_all.11 = f32[64,32,128]{2,1,0:T(8,128)S(1)} all-to-all(f32[64,32,128]{2,1,0:T(8,128)S(1)} %blend.1), channel_id=1, replica_groups=mesh['dom'=64,'lon'=4] {'dom'}, dimensions={0} | all-to-all | bytes 2097152 | tf_op jit(solution)/shard_map/all_to_all | solution.py:330
  83.8 0.0 copy-done.1
  83.8 0.0 copy-done.2
  83.8 0.6 pack.1
  84.4 5.7 %collective-permute-start.2 = (f32[128,128]{1,0:T(8,128)S(1)}, f32[128,128]{1,0:T(8,128)S(1)}, u32[]{:S(2)}, u32[]{:S(2)}) collective-permute-start(f32[128,128]{1,0:T(8,128)S(1)} %get-tuple-element.7), channel_id=1, source_target_pairs={{0,1},{1,2},{2,3},{3,0},{4,5},{5,6},{6,7},{7,4},{8,9},{9,10},{10,1... | collective-permute-start | bytes 196616 | tf_op jit(solution)/shard_map/ppermute | solution.py:318
  90.1 0.0 collective-permute-start.3
  90.1 1.3 %collective-permute-done.2.before_ref = f32[128,128]{1,0:T(8,128)S(1)} collective-permute-done((f32[128,128]{1,0:T(8,128)S(1)}, f32[128,128]{1,0:T(8,128)S(1)}, u32[]{:S(2)}, u32[]{:S(2)}) %collective-permute-start.2) | collective-permute-done | bytes 65568 | tf_op jit(solution)/shard_map/ppermute | solution.py:318
  91.5 2.4 %collective-permute-done.3.after_ref = f32[128,128]{1,0:T(8,128)S(1)} collective-permute-done((f32[128,128]{1,0:T(8,128)S(1)}, f32[128,128]{1,0:T(8,128)S(1)}, u32[]{:S(2)}, u32[]{:S(2)}) %collective-permute-start.3) | collective-permute-done | bytes 65568 | tf_op jit(solution)/shard_map/ppermute | solution.py:318
  93.8 5.4 %forecast.1 = f32[16,128,128]{2,1,0:T(8,128)} custom-call(f32[16,128,128]{2,1,0:T(8,128)S(1)} %bitcast.7, f32[4,128,128]{2,1,0:T(8,128)S(1)} %copy-done.1, s32[128,128]{1,0:T(8,128)S(1)} %copy-done.2, f32[128,128]{1,0:T(8,128)S(1)} %collective-permute-done.2.before_ref, f32[128,128]{1,0:T(8,128)S(1)} %collective-permute-done.3.after_ref), custom_call_target="tpu_custom_call" | custom-call | flops 39321600 | bytes 3145728 | tf_op jit(solution)/shard_map/forecast/pallas_call | solution.py:304
Async XLA Ops:
  0.0 4.2 %collective-permute-start.1 = (s32[2]{0:T(128)}, s32[2]{0:T(128)S(1)}, u32[]{:S(2)}, u32[]{:S(2)}) collective-permute-start(s32[2]{0:T(128)} %bitcast.11), channel_id=1, source_target_pairs={{0,3},{1,0},{2,1},{3,2},{4,7},{5,4},{6,5},{7,6},{8,11},{9,8},{10,9... | collective-permute-start | bytes 32 | tf_op jit(solution)/shard_map/ppermute | solution.py:318
  3.2 1.3 %collective-permute-start = (s32[2]{0:T(128)}, s32[2]{0:T(128)S(1)}, u32[]{:S(2)}, u32[]{:S(2)}) collective-permute-start(s32[2]{0:T(128)} %bitcast.12), channel_id=1, source_target_pairs={{0,1},{1,2},{2,3},{3,0},{4,5},{5,6},{6,7},{7,4},{8,9},{9,10},{10,1... | collective-permute-start | bytes 32 | tf_op jit(solution)/shard_map/ppermute | solution.py:318
  4.5 1.2 %copy-start = (f32[1,4,4,128,128]{4,3,2,1,0:T(8,128)S(1)}, f32[1,4,4,128,128]{4,3,2,1,0:T(8,128)}, u32[]{:S(2)}) copy-start(f32[1,4,4,128,128]{4,3,2,1,0:T(8,128)} %param.4) | copy-start | bytes 3145732
  5.7 0.7 copy-start.3
  49.7 34.1 %copy-start.1 = (f32[4,128,128]{2,1,0:T(8,128)S(1)}, f32[4,128,128]{2,1,0:T(8,128)}, u32[]{:S(2)}) copy-start(f32[4,128,128]{2,1,0:T(8,128)} %depth_ref.3) | copy-start | bytes 786436
  49.7 34.1 %copy-start.2 = (s32[128,128]{1,0:T(8,128)S(1)}, s32[128,128]{1,0:T(8,128)}, u32[]{:S(2)}) copy-start(s32[128,128]{1,0:T(8,128)} %levels_ref.3) | copy-start | bytes 196612
  84.4 7.0 %collective-permute-start.2 = (f32[128,128]{1,0:T(8,128)S(1)}, f32[128,128]{1,0:T(8,128)S(1)}, u32[]{:S(2)}, u32[]{:S(2)}) collective-permute-start(f32[128,128]{1,0:T(8,128)S(1)} %get-tuple-element.7), channel_id=1, source_target_pairs={{0,1},{1,2},{2,3},{3,0},{4,5},{5,6},{6,7},{7,4},{8,9},{9,10},{10,1... | collective-permute-start | bytes 196616 | tf_op jit(solution)/shard_map/ppermute | solution.py:318
  90.1 3.7 %collective-permute-start.3 = (f32[128,128]{1,0:T(8,128)S(1)}, f32[128,128]{1,0:T(8,128)S(1)}, u32[]{:S(2)}, u32[]{:S(2)}) collective-permute-start(f32[128,128]{1,0:T(8,128)S(1)} %get-tuple-element.8), channel_id=1, source_target_pairs={{0,3},{1,0},{2,1},{3,2},{4,7},{5,4},{6,5},{7,6},{8,11},{9,8},{10,9... | collective-permute-start | bytes 196616 | tf_op jit(solution)/shard_map/ppermute | solution.py:318

commit v3 on v2

v3 whole, which is shorter than its diff:
```python
import jax
import jax.numpy as jnp
from jax import lax
from jax.experimental import pallas as pl
from jax.experimental.pallas import tpu as pltpu
from jax.sharding import PartitionSpec as P

LEV = 4
FIELDS = 4
TILE = 64
BLEND = 8
STEPS = 3
LAT = 128
WIDTH = 128
HALO = 2 * STEPS
PAD = 8

time_step = 0.3
gravity = 1.0
drag_rate = 0.05
diffusion = 0.1
vertical_mix = 0.2
coriolis_base = 0.1
coriolis_slope = 0.3

VMEM_LIMIT = 16 * 1024 * 1024


def lanes_of(rows):
    return lax.broadcasted_iota(jnp.int32, (rows, WIDTH), 1)


def vmem(count):
    return [pl.BlockSpec(memory_space=pltpu.VMEM)] * count


def chunk_kernel(state_ref, out_ref):
    height = state_ref.shape[1]
    for chunk in range(state_ref.shape[0]):
        base = chunk * (height + 1)
        out_ref[base : base + height, :] = state_ref[chunk]


def make_chunks(chunks):
    count, height, width = chunks.shape
    shape = (count * (height + 1), width)
    return pl.pallas_call(
        chunk_kernel,
        out_shape=jax.ShapeDtypeStruct(shape, chunks.dtype),
        in_specs=vmem(1),
        out_specs=pl.BlockSpec(memory_space=pltpu.VMEM),
        compiler_params=pltpu.CompilerParams(vmem_limit_bytes=VMEM_LIMIT),
        cost_estimate=pl.CostEstimate(flops=0, bytes_accessed=8 * chunks.size, transcendentals=0),
        name="chunks",
    )(chunks)


def add_table(chunks, own, left, right, count):
    height = chunks.shape[0] // count

    def table_kernel(own_ref, left_ref, right_ref, chunks_ref, out_ref):
        del chunks_ref
        lane = lanes_of(1)
        row = jnp.zeros((1, WIDTH), jnp.int32)
        for tile, pick in enumerate((left_ref[1], own_ref[0], own_ref[1], right_ref[0])):
            row = jnp.where(lane == tile, pick, row)
        row = row.astype(jnp.float32)
        for chunk in range(count):
            base = chunk * height + height - 1
            out_ref[base : base + 1, :] = row

    return pl.pallas_call(
        table_kernel,
        out_shape=jax.ShapeDtypeStruct(chunks.shape, chunks.dtype),
        in_specs=[pl.BlockSpec(memory_space=pltpu.SMEM)] * 3 + vmem(1),
        out_specs=pl.BlockSpec(memory_space=pltpu.VMEM),
        input_output_aliases={3: 0},
        compiler_params=pltpu.CompilerParams(vmem_limit_bytes=VMEM_LIMIT),
        cost_estimate=pl.CostEstimate(flops=0, bytes_accessed=4 * count * WIDTH, transcendentals=0),
        name="table",
    )(own, left, right, chunks)


def blend_kernel(block_ref, out_ref, numbers_ref, table_ref, sem):
    particles, rows, _ = out_ref.shape
    numbers_ref[...] = block_ref[pl.ds(rows, particles, stride=rows + 1), :].astype(jnp.int32)
    copy = pltpu.make_async_copy(numbers_ref, table_ref, sem)
    copy.start()
    lane = lanes_of(8)
    position = lane % TILE
    near_left = position < BLEND
    near_right = position >= TILE - BLEND
    distance = jnp.where(near_left, position, TILE - 1 - position).astype(jnp.float32)
    weight = jnp.where(near_left | near_right, 0.5 + (distance + 0.5) / (2.0 * BLEND), 1.0)
    rest = 1.0 - weight
    first = lane < TILE
    zero = jnp.zeros_like(weight)
    weights = (
        jnp.where(first & near_left, rest, zero),
        jnp.where(first, weight, jnp.where(near_left, rest, zero)),
        jnp.where(first, jnp.where(near_right, rest, zero), weight),
        jnp.where(first, zero, jnp.where(near_right, rest, zero)),
    )
    copy.wait()

    def one(particle, carry):
        picks = [table_ref[particle, tile] * (rows + 1) for tile in range(4)]
        for row in range(0, rows, 8):
            parts = [block_ref[pl.ds(pick + row, 8), :] * w for pick, w in zip(picks, weights)]
            out_ref[particle, row : row + 8, :] = (parts[1] + parts[2]) + (parts[0] + parts[3])
        return carry

    lax.fori_loop(0, particles, one, 0, unroll=4)


def blend(block, particles):
    rows = block.shape[0] // particles - 1
    shape = (particles, rows, WIDTH)
    return pl.pallas_call(
        blend_kernel,
        out_shape=jax.ShapeDtypeStruct(shape, block.dtype),
        in_specs=vmem(1),
        out_specs=pl.BlockSpec(memory_space=pltpu.VMEM),
        scratch_shapes=[
            pltpu.VMEM((particles, WIDTH), jnp.int32),
            pltpu.SMEM((particles, WIDTH), jnp.int32),
            pltpu.SemaphoreType.DMA,
        ],
        compiler_params=pltpu.CompilerParams(vmem_limit_bytes=VMEM_LIMIT),
        cost_estimate=pl.CostEstimate(flops=4 * block.size, bytes_accessed=8 * block.size, transcendentals=0),
        name="blend",
    )(block)


def masked_thickness(depth_ref, levels_ref, level, start, rows):
    wet = levels_ref[pl.ds(start, rows), :] > level
    return jnp.where(wet, depth_ref[level, pl.ds(start, rows), :], 0.0)


def groups():
    for kind in range(FIELDS + 1):
        for level in range(LEV):
            yield kind, level, kind * 2 + level % 2, level // 2


def values_of(fields_ref, depth_ref, levels_ref, kind, level, start, rows):
    if kind < FIELDS:
        return fields_ref[kind * LEV + level, pl.ds(start, rows), :]
    return masked_thickness(depth_ref, levels_ref, level, start, rows)


def pack_kernel(fields_ref, depth_ref, levels_ref, right_ref, left_ref):
    lane = lanes_of(8)

    def within(low):
        return ((lane + (WIDTH - low)) % WIDTH) < HALO

    def one(block, carry):
        start = pl.multiple_of(block * 8, 8)
        right = jnp.zeros((8, WIDTH), jnp.float32)
        left = jnp.zeros((8, WIDTH), jnp.float32)
        for kind, level, slot, half in groups():
            values = values_of(fields_ref, depth_ref, levels_ref, kind, level, start, 8)
            low = half * TILE + HALO * slot
            turned = pltpu.roll(values, (low + HALO) % WIDTH, 1)
            right = jnp.where(within(low), turned, right)
            left = jnp.where(within(low + HALO), turned, left)
        right_ref[pl.ds(start, 8), :] = right
        left_ref[pl.ds(start, 8), :] = left
        return carry

    lax.fori_loop(0, LAT // 8, one, 0, unroll=4)


def pack(fields, depth, levels):
    shape = jax.ShapeDtypeStruct((LAT, WIDTH), jnp.float32)
    return pl.pallas_call(
        pack_kernel,
        out_shape=(shape, shape),
        in_specs=vmem(3),
        out_specs=tuple(vmem(2)),
        compiler_params=pltpu.CompilerParams(vmem_limit_bytes=VMEM_LIMIT),
        cost_estimate=pl.CostEstimate(flops=4 * fields.size, bytes_accessed=5 * fields.size, transcendentals=0),
        name="pack",
    )(fields, depth, levels)


def march(scratch, count, couple, emit):
    height, zonal, merid, tracer, thick, height_part, flux, south, north = scratch

    def rows_at(ref, which, shift):
        return ref[which, PAD + shift : PAD + LAT + shift, :]

    def put(ref, which, values):
        ref[which, PAD : PAD + LAT, :] = values

    def east(values):
        return pltpu.roll(values, WIDTH - 1, 1)

    def west(values):
        return pltpu.roll(values, 1, 1)

    edge = jnp.zeros((PAD, WIDTH), jnp.float32)
    for ref in (height, flux, south, north):
        for which in range(count):
            ref[which, 0:PAD, :] = edge
            ref[which, PAD + LAT : 2 * PAD + LAT, :] = edge

    half = 0.5 * time_step
    keep = 1.0 - time_step * drag_rate
    row = lax.broadcasted_iota(jnp.int32, (LAT, WIDTH), 0)
    turn = time_step * (coriolis_base + coriolis_slope * row.astype(jnp.float32) / LAT)

    for step in range(STEPS):
        last = step == STEPS - 1
        for which in range(count):
            h, u, v, c, t = (rows_at(ref, which, 0) for ref in (height, zonal, merid, tracer, thick))
            wet = t > 0.0
            dx = east(h) - west(h)
            dy = rows_at(height, which, 1) - rows_at(height, which, -1)
            new_u = jnp.where(wet, keep * u + turn * v - (half * gravity) * dx, 0.0)
            new_v = jnp.where(wet, keep * v - turn * u - (half * gravity) * dy, 0.0)
            some, more = diffusion * c, half * c
            along, cross = more * new_u, more * new_v
            across = t * new_u
            put(flux, which, t * new_v)
            put(south, which, some - cross)
            put(north, which, some + cross)
            if last:
                emit(1, which, new_u)
                emit(2, which, new_v)
            else:
                put(zonal, which, new_u)
                put(merid, which, new_v)
            put(height_part, which, h - half * (east(across) - west(across)))
            put(tracer, which, (1.0 - 4.0 * diffusion) * c + (east(some - along) + west(some + along)))
        moved, wets = [], []
        for which in range(count):
            wet = rows_at(thick, which, 0) > 0.0
            dy = rows_at(flux, which, 1) - rows_at(flux, which, -1)
            new_h = jnp.where(wet, rows_at(height_part, which, 0) - half * dy, 0.0)
            if last:
                emit(0, which, new_h)
            else:
                put(height, which, new_h)
            new_c = rows_at(tracer, which, 0) + (rows_at(south, which, 1) + rows_at(north, which, -1))
            moved.append(jnp.where(wet, new_c, 0.0))
            wets.append(wet)
        for which, new_c in enumerate(couple(moved, wets)):
            if last:
                emit(3, which, new_c)
            else:
                put(tracer, which, new_c)


def exchange(upper, lower, both_wet):
    return jnp.where(both_wet, vertical_mix * (lower - upper), 0.0)


def couple_levels(moved, wets):
    swaps = [exchange(moved[k], moved[k + 1], wets[k] & wets[k + 1]) for k in range(LEV - 1)]
    return [
        moved[0] + swaps[0],
        moved[1] + swaps[1] - swaps[0],
        moved[2] + swaps[2] - swaps[1],
        moved[3] - swaps[2],
    ]


def couple_pairs(moved, wets):
    even, odd = moved
    within = exchange(even, odd, wets[0] & wets[1])
    lane = lanes_of(LAT)
    wet_even = jnp.where(wets[0], 1.0, 0.0)
    turned = pltpu.roll(even, TILE, 1)
    turned_wet = pltpu.roll(wet_even, TILE, 1) > 0.0
    between = exchange(odd, turned, wets[1] & turned_wet & (lane < TILE))
    return [even + within - pltpu.roll(between, TILE, 1), odd + between - within]


def scratch_for(count):
    return [pltpu.VMEM((count, LAT + 2 * PAD, WIDTH), jnp.float32)] * 9


STRIP = 2 * HALO


def inner_kernel(fields_ref, depth_ref, levels_ref, out_ref, strip_ref, *scratch):
    lane = lanes_of(LAT)
    for kind, level, slot, half in groups():
        values = values_of(fields_ref, depth_ref, levels_ref, kind, level, 0, LAT)
        scratch[kind][level, PAD : PAD + LAT, :] = values
        base = half * TILE
        ends = jnp.where(
            lane < base + 24, pltpu.roll(values, base + STRIP, 1), pltpu.roll(values, base + 2 * STRIP, 1)
        )
        if half:
            strip_ref[slot] = jnp.where(lane < TILE, strip_ref[slot], ends)
        else:
            strip_ref[slot] = ends

    def emit(kind, level, values):
        out_ref[kind * LEV + level] = values

    march(scratch, LEV, couple_levels, emit)


def run_inner(fields, depth, levels):
    return pl.pallas_call(
        inner_kernel,
        out_shape=(
            jax.ShapeDtypeStruct(fields.shape, fields.dtype),
            jax.ShapeDtypeStruct((2 * (FIELDS + 1), LAT, WIDTH), fields.dtype),
        ),
        in_specs=vmem(3),
        out_specs=tuple(vmem(2)),
        scratch_shapes=scratch_for(LEV),
        compiler_params=pltpu.CompilerParams(vmem_limit_bytes=VMEM_LIMIT),
        cost_estimate=pl.CostEstimate(flops=75 * fields.size, bytes_accessed=12 * fields.size, transcendentals=0),
        name="inner",
    )(fields, depth, levels)


def ends_kernel(inner_ref, strip_ref, before_ref, after_ref, out_ref, *scratch):
    lane = lanes_of(LAT)
    place = lane % TILE
    in_after = (place >= STRIP) & (place < STRIP + HALO)
    in_before = (place >= STRIP + HALO) & (place < 2 * STRIP)
    before = before_ref[...]
    after = after_ref[...]
    for kind in range(FIELDS + 1):
        for which in range(2):
            slot = kind * 2 + which
            low = HALO * slot
            values = jnp.where(
                in_after,
                pltpu.roll(after, (WIDTH + STRIP - low - HALO) % WIDTH, 1),
                jnp.where(
                    in_before, pltpu.roll(before, (WIDTH + STRIP + HALO - low) % WIDTH, 1), strip_ref[slot]
                ),
            )
            scratch[kind][which, PAD : PAD + LAT, :] = values

    def emit(kind, which, values):
        for half in range(2):
            base = half * TILE
            at = kind * LEV + which + 2 * half
            last_columns = pltpu.roll(values, (WIDTH - STRIP - base) % WIDTH, 1)
            first_columns = pltpu.roll(values, (2 * WIDTH - base - 2 * STRIP) % WIDTH, 1)
            out_ref[at] = jnp.where(
                lane < HALO, first_columns, jnp.where(lane >= WIDTH - HALO, last_columns, inner_ref[at])
            )

    march(scratch, 2, couple_pairs, emit)


def run_ends(inner, strips, before, after):
    return pl.pallas_call(
        ends_kernel,
        out_shape=jax.ShapeDtypeStruct(inner.shape, inner.dtype),
        in_specs=vmem(4),
        out_specs=pl.BlockSpec(memory_space=pltpu.VMEM),
        scratch_shapes=scratch_for(2),
        compiler_params=pltpu.CompilerParams(vmem_limit_bytes=VMEM_LIMIT),
        cost_estimate=pl.CostEstimate(flops=40 * inner.size, bytes_accessed=12 * inner.size, transcendentals=0),
        name="ends",
    )(inner, strips, before, after)


def run_forecast(fields, depth, levels, before, after):
    inner, strips = run_inner(fields, depth, levels)
    return run_ends(inner, strips, before, after)


def ring(values, axis, shift):
    size = lax.axis_size(axis)
    return lax.ppermute(values, axis, [(i, (i + shift) % size) for i in range(size)])


def on_device(state, level_thickness, wet_levels, ancestors):
    size = lax.axis_size("dom")
    own = ancestors.reshape(-1)
    left = ring(own, "lon", 1)
    right = ring(own, "lon", -1)
    chunks = make_chunks(state.reshape(size, -1, WIDTH))
    chunks = add_table(chunks, own, left, right, size)
    sent = chunks.reshape(size, -1, 1, WIDTH)
    block = lax.all_to_all(sent, "dom", split_axis=0, concat_axis=0, tiled=True)
    mixed = blend(block.reshape(chunks.shape), size)
    back = lax.all_to_all(mixed, "dom", split_axis=0, concat_axis=0, tiled=True)
    fields = back.reshape(FIELDS * LEV, LAT, WIDTH)
    right, left = pack(fields, level_thickness, wet_levels)
    before = ring(right, "lon", 1)
    after = ring(left, "lon", -1)
    result = run_forecast(fields, level_thickness, wet_levels, before, after)
    return result.reshape(state.shape)


def solution(mesh):
    return jax.shard_map(
        on_device,
        mesh=mesh,
        in_specs=(
            P("dom", None, None, None, "lon"),
            P(None, None, "lon"),
            P(None, "lon"),
            P("dom", "lon", None),
        ),
        out_specs=P("dom", None, None, None, "lon"),
        check_vma=False,
    )
```

time: 99.4 us -> 95.3 us (0.959)
  waiting for transfers between devices: 4.94 us -> 0.85 us
    ppermute x4, waiting for transfers between devices: 4.94 us -> 0.85 us  [ring(): lax.ppermute(values, axis, [(i, (i + shift) % size) for i in range(size)])]
    pallas_call x1 -> x3, Pallas kernels: 5.38 us -> 6.66 us  [the longest x1 3.26 us: run_ends(): pl.pallas_call(ends_kernel, out_shape=jax.ShapeDtypeStruct(inner.shape, i...]
  transfers between devices with their start and end apart: 4 -> 4, of which waited for: 4 -> 1; matrix products, arithmetic and copies ran while one was open for 0% -> 0% of each run, Pallas kernels for 0% -> 3%
where the time goes in v3:
time: 95.3 us; the launch traced here: 95.1 us
  blocking collectives  75.2 us (79%)
  starting transfers between devices  8.92 us (9%)
  Pallas kernels  8.83 us (9%)
  local copies, waits for them, and re-layouts  1.24 us (1%)
    all_to_all x1, blocking collectives, on_device(): block = lax.all_to_all(sent, 'dom', split_axis=0, concat_axis=0, tiled=True)  41.1 us
    all_to_all x1, blocking collectives, on_device(): back = lax.all_to_all(mixed, 'dom', split_axis=0, concat_axis=0, tiled=True)  34.1 us
    ppermute x4, starting transfers between devices, ring(): lax.ppermute(values, axis, [(i, (i + shift) % size) for i in range(size)])  8.92 us
    pallas_call x1, Pallas kernels, run_ends(): pl.pallas_call(ends_kernel, out_shape=jax.ShapeDtypeStruct(inner.shape, i...  3.26 us
    pallas_call x1, Pallas kernels, run_inner(): pl.pallas_call(inner_kernel, out_shape=(jax.ShapeDtypeStruct(fields.shape...  2.83 us
  transfers between devices with their start and end apart: 4, of which 1 were waited for; matrix products, arithmetic and copies ran while one was open for 0% of the time, Pallas kernels for 3%

profile of v3, /device:TPU:1, one launch (start us, length us, event | category | flops | bytes accessed | tf_op | source)
XLA Modules:
  0.0 95.1 jit_solution(7861996038660884324)
XLA Ops:
  0.0 0.0 copy-start.3
  0.0 3.2 %collective-permute-start.1 = (s32[2]{0:T(128)}, s32[2]{0:T(128)S(1)}, u32[]{:S(2)}, u32[]{:S(2)}) collective-permute-start(s32[2]{0:T(128)} %bitcast.11), channel_id=1, source_target_pairs={{0,3},{1,0},{2,1},{3,2},{4,7},{5,4},{6,5},{7,6},{8,11},{9,8},{10,9... | collective-permute-start | bytes 32 | tf_op jit(solution)/shard_map/ppermute | solution.py:377
  3.2 0.0 collective-permute-start
  3.2 0.0 copy-start
  3.2 1.2 %copy-done = f32[1,4,4,128,128]{4,3,2,1,0:T(8,128)S(1)} copy-done((f32[1,4,4,128,128]{4,3,2,1,0:T(8,128)S(1)}, f32[1,4,4,128,128]{4,3,2,1,0:T(8,128)}, u32[]{:S(2)}) %copy-start) | copy-done | bytes 1048600
  4.5 0.1 chunks.1.chunks_ref
  4.5 0.0 collective-permute-done.1.right_ref
  4.6 0.0 collective-permute-done.left_ref
  4.6 0.0 copy-done.3
  4.6 0.6 table.1
  5.2 41.1 %all_to_all.10 = f32[64,33,1,128]{3,2,1,0:T(1,128)S(1)} all-to-all(f32[64,33,1,128]{3,2,1,0:T(1,128)S(1)} %bitcast.6), channel_id=1, replica_groups=mesh['dom'=64,'lon'=4] {'dom'}, dimensions={0} | all-to-all | bytes 2162688 | tf_op jit(solution)/shard_map/all_to_all | solution.py:388
  46.3 1.5 %blend.1 = f32[64,32,128]{2,1,0:T(8,128)S(1)} custom-call(f32[2112,128]{1,0:T(8,128)S(1)} %bitcast.9), custom_call_target="tpu_custom_call" | custom-call | flops 1081344 | bytes 2162688 | tf_op jit(solution)/shard_map/blend/pallas_call | solution.py:119
  47.8 0.0 copy-start.1
  47.8 0.0 copy-start.2
  47.8 34.1 %all_to_all.11 = f32[64,32,128]{2,1,0:T(8,128)S(1)} all-to-all(f32[64,32,128]{2,1,0:T(8,128)S(1)} %blend.1), channel_id=1, replica_groups=mesh['dom'=64,'lon'=4] {'dom'}, dimensions={0} | all-to-all | bytes 2097152 | tf_op jit(solution)/shard_map/all_to_all | solution.py:390
  81.9 0.0 copy-done.1
  81.9 0.0 copy-done.2
  81.9 0.6 pack.1
  82.5 5.7 %collective-permute-start.2 = (f32[128,128]{1,0:T(8,128)S(1)}, f32[128,128]{1,0:T(8,128)S(1)}, u32[]{:S(2)}, u32[]{:S(2)}) collective-permute-start(f32[128,128]{1,0:T(8,128)S(1)} %get-tuple-element.11), channel_id=1, source_target_pairs={{0,1},{1,2},{2,3},{3,0},{4,5},{5,6},{6,7},{7,4},{8,9},{9,10},{10,1... | collective-permute-start | bytes 196616 | tf_op jit(solution)/shard_map/ppermute | solution.py:377
  88.2 0.0 collective-permute-start.3
  88.2 2.8 %inner.1 = (f32[16,128,128]{2,1,0:T(8,128)S(1)}, f32[10,128,128]{2,1,0:T(8,128)S(1)}) custom-call(f32[16,128,128]{2,1,0:T(8,128)S(1)} %bitcast.8, f32[4,128,128]{2,1,0:T(8,128)S(1)} %copy-done.1, s32[128,128]{1,0:T(8,128)S(1)} %copy-done.2), custom_call_target="tpu_custom_call" | custom-call | flops 19660800 | bytes 3145728 | tf_op jit(solution)/shard_map/inner/pallas_call | solution.py:309
  91.0 0.0 collective-permute-done.2.before_ref
  91.0 0.8 collective-permute-done.3.after_ref
  91.9 3.3 %ends.1 = f32[16,128,128]{2,1,0:T(8,128)} custom-call(f32[16,128,128]{2,1,0:T(8,128)S(1)} %get-tuple-element.9.inner_ref, f32[10,128,128]{2,1,0:T(8,128)S(1)} %get-tuple-element.10.strip_ref, f32[128,128]{1,0:T(8,128)S(1)} %collective-permute-done.2.before_ref, f32[128,128]{1,0:T(8,128)S(1)} %collective-permute-done.3.after_ref), custom_call_target="tpu_custom_call" | custom-call | flops 10485760 | bytes 3145728 | tf_op jit(solution)/shard_map/ends/pallas_call | solution.py:358
Async XLA Ops:
  0.0 4.6 %copy-start.3 = (s32[1,2,1]{1,2,0:T(1,128)S(1)}, s32[1,2,1]{1,2,0:T(1,128)}, u32[]{:S(2)}) copy-start(s32[1,2,1]{1,2,0:T(1,128)} %param.7) | copy-start | bytes 28
  0.0 4.5 %collective-permute-start.1 = (s32[2]{0:T(128)}, s32[2]{0:T(128)S(1)}, u32[]{:S(2)}, u32[]{:S(2)}) collective-permute-start(s32[2]{0:T(128)} %bitcast.11), channel_id=1, source_target_pairs={{0,3},{1,0},{2,1},{3,2},{4,7},{5,4},{6,5},{7,6},{8,11},{9,8},{10,9... | collective-permute-start | bytes 32 | tf_op jit(solution)/shard_map/ppermute | solution.py:377
  3.2 1.3 %collective-permute-start = (s32[2]{0:T(128)}, s32[2]{0:T(128)S(1)}, u32[]{:S(2)}, u32[]{:S(2)}) collective-permute-start(s32[2]{0:T(128)} %bitcast.12), channel_id=1, source_target_pairs={{0,1},{1,2},{2,3},{3,0},{4,5},{5,6},{6,7},{7,4},{8,9},{9,10},{10,1... | collective-permute-start | bytes 32 | tf_op jit(solution)/shard_map/ppermute | solution.py:377
  3.2 1.2 %copy-start = (f32[1,4,4,128,128]{4,3,2,1,0:T(8,128)S(1)}, f32[1,4,4,128,128]{4,3,2,1,0:T(8,128)}, u32[]{:S(2)}) copy-start(f32[1,4,4,128,128]{4,3,2,1,0:T(8,128)} %param.4) | copy-start | bytes 3145732
  47.8 34.1 %copy-start.1 = (f32[4,128,128]{2,1,0:T(8,128)S(1)}, f32[4,128,128]{2,1,0:T(8,128)}, u32[]{:S(2)}) copy-start(f32[4,128,128]{2,1,0:T(8,128)} %depth_ref.3) | copy-start | bytes 786436
  47.8 34.1 %copy-start.2 = (s32[128,128]{1,0:T(8,128)S(1)}, s32[128,128]{1,0:T(8,128)}, u32[]{:S(2)}) copy-start(s32[128,128]{1,0:T(8,128)} %levels_ref.3) | copy-start | bytes 196612
  82.5 8.5 %collective-permute-start.2 = (f32[128,128]{1,0:T(8,128)S(1)}, f32[128,128]{1,0:T(8,128)S(1)}, u32[]{:S(2)}, u32[]{:S(2)}) collective-permute-start(f32[128,128]{1,0:T(8,128)S(1)} %get-tuple-element.11), channel_id=1, source_target_pairs={{0,1},{1,2},{2,3},{3,0},{4,5},{5,6},{6,7},{7,4},{8,9},{9,10},{10,1... | collective-permute-start | bytes 196616 | tf_op jit(solution)/shard_map/ppermute | solution.py:377
  88.2 3.7 %collective-permute-start.3 = (f32[128,128]{1,0:T(8,128)S(1)}, f32[128,128]{1,0:T(8,128)S(1)}, u32[]{:S(2)}, u32[]{:S(2)}) collective-permute-start(f32[128,128]{1,0:T(8,128)S(1)} %get-tuple-element.12), channel_id=1, source_target_pairs={{0,3},{1,0},{2,1},{3,2},{4,7},{5,4},{6,5},{7,6},{8,11},{9,8},{10,9... | collective-permute-start | bytes 196616 | tf_op jit(solution)/shard_map/ppermute | solution.py:377

commit v4 on v3

--- a/solution.py
+++ b/solution.py
@@ -60,10 +60,11 @@
 
     def table_kernel(own_ref, left_ref, right_ref, chunks_ref, out_ref):
         del chunks_ref
-        lane = lanes_of(1)
+        tile = lanes_of(1) % 4
+        picks = (left_ref[0:1, 1:2], own_ref[0:1, 0:1], own_ref[0:1, 1:2], right_ref[0:1, 0:1])
         row = jnp.zeros((1, WIDTH), jnp.int32)
-        for tile, pick in enumerate((left_ref[1], own_ref[0], own_ref[1], right_ref[0])):
-            row = jnp.where(lane == tile, pick, row)
+        for at, pick in enumerate(picks):
+            row = jnp.where(tile == at, pick, row)
         row = row.astype(jnp.float32)
         for chunk in range(count):
             base = chunk * height + height - 1
@@ -72,7 +73,7 @@
     return pl.pallas_call(
         table_kernel,
         out_shape=jax.ShapeDtypeStruct(chunks.shape, chunks.dtype),
-        in_specs=[pl.BlockSpec(memory_space=pltpu.SMEM)] * 3 + vmem(1),
+        in_specs=vmem(4),
         out_specs=pl.BlockSpec(memory_space=pltpu.VMEM),
         input_output_aliases={3: 0},
         compiler_params=pltpu.CompilerParams(vmem_limit_bytes=VMEM_LIMIT),
@@ -81,9 +82,17 @@
     )(own, left, right, chunks)
 
 
+SHARE = WIDTH // 4
+
+
 def blend_kernel(block_ref, out_ref, numbers_ref, table_ref, sem):
     particles, rows, _ = out_ref.shape
-    numbers_ref[...] = block_ref[pl.ds(rows, particles, stride=rows + 1), :].astype(jnp.int32)
+    table = block_ref[pl.ds(rows, particles, stride=rows + 1), :]
+    holder = lax.broadcasted_iota(jnp.int32, (particles, WIDTH), 0) % SHARE
+    table = jnp.where(lanes_of(particles) // 4 == holder, table, 0.0)
+    for line in range(particles // SHARE):
+        total = jnp.sum(table[line * SHARE : (line + 1) * SHARE], axis=0, keepdims=True)
+        numbers_ref[line : line + 1, :] = total.astype(jnp.int32)
     copy = pltpu.make_async_copy(numbers_ref, table_ref, sem)
     copy.start()
     lane = lanes_of(8)
@@ -104,7 +113,8 @@
     copy.wait()
 
     def one(particle, carry):
-        picks = [table_ref[particle, tile] * (rows + 1) for tile in range(4)]
+        line, first_tile = particle // SHARE, 4 * (particle % SHARE)
+        picks = [table_ref[line, first_tile + tile] * (rows + 1) for tile in range(4)]
         for row in range(0, rows, 8):
             parts = [block_ref[pl.ds(pick + row, 8), :] * w for pick, w in zip(picks, weights)]
             out_ref[particle, row : row + 8, :] = (parts[1] + parts[2]) + (parts[0] + parts[3])
@@ -122,8 +132,8 @@
         in_specs=vmem(1),
         out_specs=pl.BlockSpec(memory_space=pltpu.VMEM),
         scratch_shapes=[
-            pltpu.VMEM((particles, WIDTH), jnp.int32),
-            pltpu.SMEM((particles, WIDTH), jnp.int32),
+            pltpu.VMEM((particles // SHARE, WIDTH), jnp.int32),
+            pltpu.SMEM((particles // SHARE, WIDTH), jnp.int32),
             pltpu.SemaphoreType.DMA,
         ],
         compiler_params=pltpu.CompilerParams(vmem_limit_bytes=VMEM_LIMIT),
@@ -150,26 +160,22 @@
 
 
 def pack_kernel(fields_ref, depth_ref, levels_ref, right_ref, left_ref):
-    lane = lanes_of(8)
+    lane = lanes_of(PROWS)
 
     def within(low):
         return ((lane + (WIDTH - low)) % WIDTH) < HALO
 
-    def one(block, carry):
-        start = pl.multiple_of(block * 8, 8)
-        right = jnp.zeros((8, WIDTH), jnp.float32)
-        left = jnp.zeros((8, WIDTH), jnp.float32)
+    for start in range(0, LAT, PROWS):
+        right = jnp.zeros((PROWS, WIDTH), jnp.float32)
+        left = jnp.zeros((PROWS, WIDTH), jnp.float32)
         for kind, level, slot, half in groups():
-            values = values_of(fields_ref, depth_ref, levels_ref, kind, level, start, 8)
+            values = values_of(fields_ref, depth_ref, levels_ref, kind, level, start, PROWS)
             low = half * TILE + HALO * slot
             turned = pltpu.roll(values, (low + HALO) % WIDTH, 1)
             right = jnp.where(within(low), turned, right)
             left = jnp.where(within(low + HALO), turned, left)
-        right_ref[pl.ds(start, 8), :] = right
-        left_ref[pl.ds(start, 8), :] = left
-        return carry
-
-    lax.fori_loop(0, LAT // 8, one, 0, unroll=4)
+        right_ref[start : start + PROWS, :] = right
+        left_ref[start : start + PROWS, :] = left
 
 
 def pack(fields, depth, levels):
@@ -185,72 +191,69 @@
     )(fields, depth, levels)
 
 
-def march(scratch, count, couple, emit):
-    height, zonal, merid, tracer, thick, height_part, flux, south, north = scratch
-
-    def rows_at(ref, which, shift):
-        return ref[which, PAD + shift : PAD + LAT + shift, :]
-
-    def put(ref, which, values):
-        ref[which, PAD : PAD + LAT, :] = values
+def march(scratch, count, couple, emit, winds_done=lambda: None):
+    height, zonal, merid, tracer, thick, flux, south, north = scratch
+
+    def rows_at(ref, shift):
+        return ref[:, PAD + shift : PAD + LAT + shift, :]
+
+    def put(ref, values):
+        ref[:, PAD : PAD + LAT, :] = values
 
     def east(values):
-        return pltpu.roll(values, WIDTH - 1, 1)
+        return pltpu.roll(values, WIDTH - 1, 2)
 
     def west(values):
-        return pltpu.roll(values, 1, 1)
-
-    edge = jnp.zeros((PAD, WIDTH), jnp.float32)
+        return pltpu.roll(values, 1, 2)
+
+    edge = jnp.zeros((count, PAD, WIDTH), jnp.float32)
     for ref in (height, flux, south, north):
-        for which in range(count):
-            ref[which, 0:PAD, :] = edge
-            ref[which, PAD + LAT : 2 * PAD + LAT, :] = edge
+        ref[:, 0:PAD, :] = edge
+        ref[:, PAD + LAT : 2 * PAD + LAT, :] = edge
 
     half = 0.5 * time_step
     keep = 1.0 - time_step * drag_rate
     row = lax.broadcasted_iota(jnp.int32, (LAT, WIDTH), 0)
     turn = time_step * (coriolis_base + coriolis_slope * row.astype(jnp.float32) / LAT)
+    turn = turn[None]
 
     for step in range(STEPS):
         last = step == STEPS - 1
+        h, u, v, c, t = (rows_at(ref, 0) for ref in (height, zonal, merid, tracer, thick))
+        wet = t > 0.0
+        dx = east(h) - west(h)
+        dy = rows_at(height, 1) - rows_at(height, -1)
+        new_u = jnp.where(wet, keep * u + turn * v - (half * gravity) * dx, 0.0)
+        new_v = jnp.where(wet, keep * v - turn * u - (half * gravity) * dy, 0.0)
+        some, more = diffusion * c, half * c
+        along, cross = more * new_u, more * new_v
+        across = t * new_u
+        put(flux, t * new_v)
+        put(south, some - cross)
+        put(north, some + cross)
+        if last:
+            for which in range(count):
+                emit(1, which, new_u[which])
+                emit(2, which, new_v[which])
+            winds_done()
+        else:
+            put(zonal, new_u)
+            put(merid, new_v)
+        part = h - half * (east(across) - west(across))
+        c_part = (1.0 - 4.0 * diffusion) * c + (east(some - along) + west(some + along))
+        dy = rows_at(flux, 1) - rows_at(flux, -1)
+        new_h = jnp.where(wet, part - half * dy, 0.0)
+        new_c = jnp.where(wet, c_part + (rows_at(south, 1) + rows_at(north, -1)), 0.0)
+        moved = [new_c[which] for which in range(count)]
+        wets = [wet[which] for which in range(count)]
+        coupled = couple(moved, wets)
         for which in range(count):
-            h, u, v, c, t = (rows_at(ref, which, 0) for ref in (height, zonal, merid, tracer, thick))
-            wet = t > 0.0
-            dx = east(h) - west(h)
-            dy = rows_at(height, which, 1) - rows_at(height, which, -1)
-            new_u = jnp.where(wet, keep * u + turn * v - (half * gravity) * dx, 0.0)
-            new_v = jnp.where(wet, keep * v - turn * u - (half * gravity) * dy, 0.0)
-            some, more = diffusion * c, half * c
-            along, cross = more * new_u, more * new_v
-            across = t * new_u
-            put(flux, which, t * new_v)
-            put(south, which, some - cross)
-            put(north, which, some + cross)
             if last:
-                emit(1, which, new_u)
-                emit(2, which, new_v)
+                emit(0, which, new_h[which])
+                emit(3, which, coupled[which])
             else:
-                put(zonal, which, new_u)
-                put(merid, which, new_v)
-            put(height_part, which, h - half * (east(across) - west(across)))
-            put(tracer, which, (1.0 - 4.0 * diffusion) * c + (east(some - along) + west(some + along)))
-        moved, wets = [], []
-        for which in range(count):
-            wet = rows_at(thick, which, 0) > 0.0
-            dy = rows_at(flux, which, 1) - rows_at(flux, which, -1)
-            new_h = jnp.where(wet, rows_at(height_part, which, 0) - half * dy, 0.0)
-            if last:
-                emit(0, which, new_h)
-            else:
-                put(height, which, new_h)
-            new_c = rows_at(tracer, which, 0) + (rows_at(south, which, 1) + rows_at(north, which, -1))
-            moved.append(jnp.where(wet, new_c, 0.0))
-            wets.append(wet)
-        for which, new_c in enumerate(couple(moved, wets)):
-            if last:
-                emit(3, which, new_c)
-            else:
-                put(tracer, which, new_c)
+                height[which, PAD : PAD + LAT, :] = new_h[which]
+                tracer[which, PAD : PAD + LAT, :] = coupled[which]
 
 
 def exchange(upper, lower, both_wet):
@@ -279,10 +282,11 @@
 
 
 def scratch_for(count):
-    return [pltpu.VMEM((count, LAT + 2 * PAD, WIDTH), jnp.float32)] * 9
+    return [pltpu.VMEM((count, LAT + 2 * PAD, WIDTH), jnp.float32)] * 8
 
 
 STRIP = 2 * HALO
+PROWS = 128
 
 
 def inner_kernel(fields_ref, depth_ref, levels_ref, out_ref, strip_ref, *scratch):
@@ -321,7 +325,7 @@
     )(fields, depth, levels)
 
 
-def ends_kernel(inner_ref, strip_ref, before_ref, after_ref, out_ref, *scratch):
+def ends_kernel(inner_ref, strip_ref, before_ref, after_ref, out_ref, result_ref, sems, *scratch):
     lane = lanes_of(LAT)
     place = lane % TILE
     in_after = (place >= STRIP) & (place < STRIP + HALO)
@@ -347,11 +351,26 @@
             at = kind * LEV + which + 2 * half
             last_columns = pltpu.roll(values, (WIDTH - STRIP - base) % WIDTH, 1)
             first_columns = pltpu.roll(values, (2 * WIDTH - base - 2 * STRIP) % WIDTH, 1)
-            out_ref[at] = jnp.where(
+            result_ref[at] = jnp.where(
                 lane < HALO, first_columns, jnp.where(lane >= WIDTH - HALO, last_columns, inner_ref[at])
             )
 
-    march(scratch, 2, couple_pairs, emit)
+    copies = [
+        pltpu.make_async_copy(
+            result_ref.at[kind * LEV : kind * LEV + LEV], out_ref.at[kind * LEV : kind * LEV + LEV], sems.at[kind]
+        )
+        for kind in range(FIELDS)
+    ]
+
+    def winds_done():
+        copies[1].start()
+        copies[2].start()
+
+    march(scratch, 2, couple_pairs, emit, winds_done)
+    copies[0].start()
+    copies[3].start()
+    for copy in copies:
+        copy.wait()
 
 
 def run_ends(inner, strips, before, after):
@@ -359,8 +378,8 @@
         ends_kernel,
         out_shape=jax.ShapeDtypeStruct(inner.shape, inner.dtype),
         in_specs=vmem(4),
-        out_specs=pl.BlockSpec(memory_space=pltpu.VMEM),
-        scratch_shapes=scratch_for(2),
+        out_specs=pl.BlockSpec(memory_space=pl.ANY),
+        scratch_shapes=[pltpu.VMEM(inner.shape, inner.dtype), pltpu.SemaphoreType.DMA((FIELDS,))] + scratch_for(2),
         compiler_params=pltpu.CompilerParams(vmem_limit_bytes=VMEM_LIMIT),
         cost_estimate=pl.CostEstimate(flops=40 * inner.size, bytes_accessed=12 * inner.size, transcendentals=0),
         name="ends",
@@ -379,7 +398,7 @@
 
 def on_device(state, level_thickness, wet_levels, ancestors):
     size = lax.axis_size("dom")
-    own = ancestors.reshape(-1)
+    own = ancestors.reshape(1, -1)
     left = ring(own, "lon", 1)
     right = ring(own, "lon", -1)
     chunks = make_chunks(state.reshape(size, -1, WIDTH))

time: 95.3 us -> 94.5 us (level)
  Pallas kernels: 8.83 us -> 7.64 us
where the time goes in v4:
time: 94.5 us; the launch traced here: 94.3 us
  blocking collectives  75.2 us (80%)
  starting transfers between devices  8.92 us (9%)
  Pallas kernels  7.64 us (8%)
  waiting for transfers between devices  1.25 us (1%)
  local copies, waits for them, and re-layouts  1.24 us (1%)
    all_to_all x1, blocking collectives, on_device(): block = lax.all_to_all(sent, 'dom', split_axis=0, concat_axis=0, tiled=True)  41.1 us
    all_to_all x1, blocking collectives, on_device(): back = lax.all_to_all(mixed, 'dom', split_axis=0, concat_axis=0, tiled=True)  34.1 us
    ppermute x4, starting transfers between devices, ring(): lax.ppermute(values, axis, [(i, (i + shift) % size) for i in range(size)])  8.92 us
    pallas_call x1, Pallas kernels, run_ends(): pl.pallas_call(ends_kernel, out_shape=jax.ShapeDtypeStruct(inner.shape, i...  2.99 us
    pallas_call x1, Pallas kernels, run_inner(): pl.pallas_call(inner_kernel, out_shape=(jax.ShapeDtypeStruct(fields.shape...  2.43 us
  transfers between devices with their start and end apart: 4, of which 1 were waited for; matrix products, arithmetic and copies ran while one was open for 0% of the time, Pallas kernels for 3%

profile of v4, /device:TPU:1, one launch (start us, length us, event | category | flops | bytes accessed | tf_op | source)
XLA Modules:
  0.0 94.3 jit_solution(13310272232408125819)
XLA Ops:
  0.0 0.0 copy-start.3
  0.0 3.2 %collective-permute-start.1 = (s32[1,2]{1,0:T(1,128)}, s32[1,2]{1,0:T(1,128)S(1)}, u32[]{:S(2)}, u32[]{:S(2)}) collective-permute-start(s32[1,2]{1,0:T(1,128)} %bitcast.11), channel_id=1, source_target_pairs={{0,3},{1,0},{2,1},{3,2},{4,7},{5,4},{6,5},{7,6},{8,11},{9,8},{10,9... | collective-permute-start | bytes 32 | tf_op jit(solution)/shard_map/ppermute | solution.py:396
  3.2 0.0 collective-permute-start
  3.2 0.0 copy-start
  3.2 1.2 %copy-done = f32[1,4,4,128,128]{4,3,2,1,0:T(8,128)S(1)} copy-done((f32[1,4,4,128,128]{4,3,2,1,0:T(8,128)S(1)}, f32[1,4,4,128,128]{4,3,2,1,0:T(8,128)}, u32[]{:S(2)}) %copy-start) | copy-done | bytes 1048600
  4.5 0.1 chunks.1.chunks_ref
  4.5 0.0 collective-permute-done.1.right_ref
  4.6 0.0 collective-permute-done.left_ref
  4.6 0.0 copy-done.3
  4.6 0.1 table.1
  4.7 41.1 %all_to_all.10 = f32[64,33,1,128]{3,2,1,0:T(1,128)S(1)} all-to-all(f32[64,33,1,128]{3,2,1,0:T(1,128)S(1)} %bitcast.6), channel_id=1, replica_groups=mesh['dom'=64,'lon'=4] {'dom'}, dimensions={0} | all-to-all | bytes 2162688 | tf_op jit(solution)/shard_map/all_to_all | solution.py:407
  45.8 1.7 %blend.1 = f32[64,32,128]{2,1,0:T(8,128)S(1)} custom-call(f32[2112,128]{1,0:T(8,128)S(1)} %bitcast.9), custom_call_target="tpu_custom_call" | custom-call | flops 1081344 | bytes 2162688 | tf_op jit(solution)/shard_map/blend/pallas_call | solution.py:129
  47.5 0.0 copy-start.1
  47.5 0.0 copy-start.2
  47.5 34.1 %all_to_all.11 = f32[64,32,128]{2,1,0:T(8,128)S(1)} all-to-all(f32[64,32,128]{2,1,0:T(8,128)S(1)} %blend.1), channel_id=1, replica_groups=mesh['dom'=64,'lon'=4] {'dom'}, dimensions={0} | all-to-all | bytes 2097152 | tf_op jit(solution)/shard_map/all_to_all | solution.py:409
  81.6 0.0 copy-done.1
  81.6 0.0 copy-done.2
  81.6 0.4 pack.1
  82.0 5.7 %collective-permute-start.2 = (f32[128,128]{1,0:T(8,128)S(1)}, f32[128,128]{1,0:T(8,128)S(1)}, u32[]{:S(2)}, u32[]{:S(2)}) collective-permute-start(f32[128,128]{1,0:T(8,128)S(1)} %get-tuple-element.11), channel_id=1, source_target_pairs={{0,1},{1,2},{2,3},{3,0},{4,5},{5,6},{6,7},{7,4},{8,9},{9,10},{10,1... | collective-permute-start | bytes 196616 | tf_op jit(solution)/shard_map/ppermute | solution.py:396
  87.7 0.0 collective-permute-start.3
  87.7 2.4 %inner.1 = (f32[16,128,128]{2,1,0:T(8,128)S(1)}, f32[10,128,128]{2,1,0:T(8,128)S(1)}) custom-call(f32[16,128,128]{2,1,0:T(8,128)S(1)} %bitcast.8, f32[4,128,128]{2,1,0:T(8,128)S(1)} %copy-done.1, s32[128,128]{1,0:T(8,128)S(1)} %copy-done.2), custom_call_target="tpu_custom_call" | custom-call | flops 19660800 | bytes 3145728 | tf_op jit(solution)/shard_map/inner/pallas_call | solution.py:313
  90.1 0.0 collective-permute-done.2.before_ref
  90.1 1.2 %collective-permute-done.3.after_ref = f32[128,128]{1,0:T(8,128)S(1)} collective-permute-done((f32[128,128]{1,0:T(8,128)S(1)}, f32[128,128]{1,0:T(8,128)S(1)}, u32[]{:S(2)}, u32[]{:S(2)}) %collective-permute-start.3) | collective-permute-done | bytes 65568 | tf_op jit(solution)/shard_map/ppermute | solution.py:396
  91.3 3.0 %ends.1 = f32[16,128,128]{2,1,0:T(8,128)} custom-call(f32[16,128,128]{2,1,0:T(8,128)S(1)} %get-tuple-element.9.inner_ref, f32[10,128,128]{2,1,0:T(8,128)S(1)} %get-tuple-element.10.strip_ref, f32[128,128]{1,0:T(8,128)S(1)} %collective-permute-done.2.before_ref, f32[128,128]{1,0:T(8,128)S(1)} %collective-permute-done.3.after_ref), custom_call_target="tpu_custom_call" | custom-call | flops 10485760 | bytes 3145728 | tf_op jit(solution)/shard_map/ends/pallas_call | solution.py:377
Async XLA Ops:
  0.0 4.6 %copy-start.3 = (s32[1,2,1]{1,2,0:T(1,128)S(1)}, s32[1,2,1]{1,2,0:T(1,128)}, u32[]{:S(2)}) copy-start(s32[1,2,1]{1,2,0:T(1,128)} %param.7) | copy-start | bytes 28
  0.0 4.5 %collective-permute-start.1 = (s32[1,2]{1,0:T(1,128)}, s32[1,2]{1,0:T(1,128)S(1)}, u32[]{:S(2)}, u32[]{:S(2)}) collective-permute-start(s32[1,2]{1,0:T(1,128)} %bitcast.11), channel_id=1, source_target_pairs={{0,3},{1,0},{2,1},{3,2},{4,7},{5,4},{6,5},{7,6},{8,11},{9,8},{10,9... | collective-permute-start | bytes 32 | tf_op jit(solution)/shard_map/ppermute | solution.py:396
  3.2 1.3 %collective-permute-start = (s32[1,2]{1,0:T(1,128)}, s32[1,2]{1,0:T(1,128)S(1)}, u32[]{:S(2)}, u32[]{:S(2)}) collective-permute-start(s32[1,2]{1,0:T(1,128)} %bitcast.12), channel_id=1, source_target_pairs={{0,1},{1,2},{2,3},{3,0},{4,5},{5,6},{6,7},{7,4},{8,9},{9,10},{10,1... | collective-permute-start | bytes 32 | tf_op jit(solution)/shard_map/ppermute | solution.py:396
  3.2 1.2 %copy-start = (f32[1,4,4,128,128]{4,3,2,1,0:T(8,128)S(1)}, f32[1,4,4,128,128]{4,3,2,1,0:T(8,128)}, u32[]{:S(2)}) copy-start(f32[1,4,4,128,128]{4,3,2,1,0:T(8,128)} %param.4) | copy-start | bytes 3145732
  47.5 34.1 %copy-start.1 = (f32[4,128,128]{2,1,0:T(8,128)S(1)}, f32[4,128,128]{2,1,0:T(8,128)}, u32[]{:S(2)}) copy-start(f32[4,128,128]{2,1,0:T(8,128)} %depth_ref.3) | copy-start | bytes 786436
  47.5 34.1 %copy-start.2 = (s32[128,128]{1,0:T(8,128)S(1)}, s32[128,128]{1,0:T(8,128)}, u32[]{:S(2)}) copy-start(s32[128,128]{1,0:T(8,128)} %levels_ref.3) | copy-start | bytes 196612
  82.0 8.1 %collective-permute-start.2 = (f32[128,128]{1,0:T(8,128)S(1)}, f32[128,128]{1,0:T(8,128)S(1)}, u32[]{:S(2)}, u32[]{:S(2)}) collective-permute-start(f32[128,128]{1,0:T(8,128)S(1)} %get-tuple-element.11), channel_id=1, source_target_pairs={{0,1},{1,2},{2,3},{3,0},{4,5},{5,6},{6,7},{7,4},{8,9},{9,10},{10,1... | collective-permute-start | bytes 196616 | tf_op jit(solution)/shard_map/ppermute | solution.py:396
  87.7 3.7 %collective-permute-start.3 = (f32[128,128]{1,0:T(8,128)S(1)}, f32[128,128]{1,0:T(8,128)S(1)}, u32[]{:S(2)}, u32[]{:S(2)}) collective-permute-start(f32[128,128]{1,0:T(8,128)S(1)} %get-tuple-element.12), channel_id=1, source_target_pairs={{0,3},{1,0},{2,1},{3,2},{4,7},{5,4},{6,5},{7,6},{8,11},{9,8},{10,9... | collective-permute-start | bytes 196616 | tf_op jit(solution)/shard_map/ppermute | solution.py:396

commit v5 on v4

--- a/solution.py
+++ b/solution.py
@@ -13,6 +13,8 @@
 LAT = 128
 WIDTH = 128
 HALO = 2 * STEPS
+DOM = (2, 4, 8)
+HOP = (1, 2, 4)
 PAD = 8
 
 time_step = 0.3
@@ -55,11 +57,11 @@
     )(chunks)
 
 
-def add_table(chunks, own, left, right, count):
+def add_table(chunks, own, left, right, turn, count):
     height = chunks.shape[0] // count
 
-    def table_kernel(own_ref, left_ref, right_ref, chunks_ref, out_ref):
-        del chunks_ref
+    def table_kernel(own_ref, left_ref, right_ref, turn_ref, chunks_ref, out_ref):
+        del turn_ref, chunks_ref
         tile = lanes_of(1) % 4
         picks = (left_ref[0:1, 1:2], own_ref[0:1, 0:1], own_ref[0:1, 1:2], right_ref[0:1, 0:1])
         row = jnp.zeros((1, WIDTH), jnp.int32)
@@ -73,16 +75,19 @@
     return pl.pallas_call(
         table_kernel,
         out_shape=jax.ShapeDtypeStruct(chunks.shape, chunks.dtype),
-        in_specs=vmem(4),
+        in_specs=vmem(5),
         out_specs=pl.BlockSpec(memory_space=pltpu.VMEM),
-        input_output_aliases={3: 0},
+        input_output_aliases={4: 0},
         compiler_params=pltpu.CompilerParams(vmem_limit_bytes=VMEM_LIMIT),
         cost_estimate=pl.CostEstimate(flops=0, bytes_accessed=4 * count * WIDTH, transcendentals=0),
         name="table",
-    )(own, left, right, chunks)
+    )(own, left, right, turn, chunks)
 
 
 SHARE = WIDTH // 4
+TOGETHER = 8
+BROWS = 32
+UNROLL = 2
 
 
 def blend_kernel(block_ref, out_ref, numbers_ref, table_ref, sem):
@@ -95,7 +100,7 @@
         numbers_ref[line : line + 1, :] = total.astype(jnp.int32)
     copy = pltpu.make_async_copy(numbers_ref, table_ref, sem)
     copy.start()
-    lane = lanes_of(8)
+    lane = lanes_of(BROWS)
     position = lane % TILE
     near_left = position < BLEND
     near_right = position >= TILE - BLEND
@@ -112,15 +117,20 @@
     )
     copy.wait()
 
-    def one(particle, carry):
-        line, first_tile = particle // SHARE, 4 * (particle % SHARE)
-        picks = [table_ref[line, first_tile + tile] * (rows + 1) for tile in range(4)]
-        for row in range(0, rows, 8):
-            parts = [block_ref[pl.ds(pick + row, 8), :] * w for pick, w in zip(picks, weights)]
-            out_ref[particle, row : row + 8, :] = (parts[1] + parts[2]) + (parts[0] + parts[3])
+    def some(at, carry):
+        done = []
+        for particle in range(TOGETHER):
+            particle = at * TOGETHER + particle
+            line, first_tile = particle // SHARE, 4 * (particle % SHARE)
+            picks = [table_ref[line, first_tile + tile] * (rows + 1) for tile in range(4)]
+            for row in range(0, rows, BROWS):
+                parts = [block_ref[pl.ds(pick + row, BROWS), :] * w for pick, w in zip(picks, weights)]
+                done.append((particle, row, (parts[1] + parts[2]) + (parts[0] + parts[3])))
+        for particle, row, values in done:
+            out_ref[particle, row : row + BROWS, :] = values
         return carry
 
-    lax.fori_loop(0, particles, one, 0, unroll=4)
+    lax.fori_loop(0, particles // TOGETHER, some, 0, unroll=UNROLL)
 
 
 def blend(block, particles):
@@ -396,13 +406,27 @@
     return lax.ppermute(values, axis, [(i, (i + shift) % size) for i in range(size)])
 
 
+def take_turns(values):
+    bands = lax.axis_size("lon")
+    halves, columns, layers = DOM
+    pairs = []
+    for here in range(halves * columns * layers):
+        half, column, layer = here // (columns * layers), here // layers % columns, here % layers
+        there = (half + HOP[0]) % halves
+        there = there * columns + (column + HOP[1]) % columns
+        there = there * layers + (layer + HOP[2]) % layers
+        pairs += [(here * bands + band, there * bands + band) for band in range(1, bands, 2)]
+    return lax.ppermute(values, ("dom", "lon"), pairs)
+
+
 def on_device(state, level_thickness, wet_levels, ancestors):
     size = lax.axis_size("dom")
     own = ancestors.reshape(1, -1)
     left = ring(own, "lon", 1)
     right = ring(own, "lon", -1)
     chunks = make_chunks(state.reshape(size, -1, WIDTH))
-    chunks = add_table(chunks, own, left, right, size)
+    left, right = lax.optimization_barrier((left, right))
+    chunks = add_table(chunks, own, left, right, take_turns(left), size)
     sent = chunks.reshape(size, -1, 1, WIDTH)
     block = lax.all_to_all(sent, "dom", split_axis=0, concat_axis=0, tiled=True)
     mixed = blend(block.reshape(chunks.shape), size)

time: 94.5 us -> 89 us (0.942)
  blocking collectives: 75.2 us -> 61 us
  starting transfers between devices: 8.92 us -> 17.1 us
    ppermute x0 -> x1, starting transfers between devices: none -> 13.3 us  [take_turns(): return lax.ppermute(values, ('dom', 'lon'), pairs)]
    all_to_all x1, blocking collectives: 41.1 us -> 33.2 us  [on_device(): block = lax.all_to_all(sent, 'dom', split_axis=0, concat_axis=0, tiled=True)]
    all_to_all x1, blocking collectives: 34.1 us -> 27.8 us  [on_device(): back = lax.all_to_all(mixed, 'dom', split_axis=0, concat_axis=0, tiled=True)]
    ppermute x4, starting transfers between devices: 8.92 us -> 3.82 us  [ring(): lax.ppermute(values, axis, [(i, (i + shift) % size) for i in range(size)])]
  transfers between devices with their start and end apart: 4 -> 5, of which waited for: 1 -> 2; matrix products, arithmetic and copies ran while one was open for 0% -> 0% of each run, Pallas kernels for 3% -> 3%
where the time goes in v5:
time: 89 us; the launch traced here: 88.7 us
  blocking collectives  61 us (69%)
  starting transfers between devices  17.1 us (19%)
  Pallas kernels  7.54 us (8%)
  waiting for transfers between devices  1.74 us (2%)
  local copies, waits for them, and re-layouts  1.24 us (1%)
    all_to_all x1, blocking collectives, on_device(): block = lax.all_to_all(sent, 'dom', split_axis=0, concat_axis=0, tiled=True)  33.2 us
    all_to_all x1, blocking collectives, on_device(): back = lax.all_to_all(mixed, 'dom', split_axis=0, concat_axis=0, tiled=True)  27.8 us
    ppermute x1, starting transfers between devices, take_turns(): return lax.ppermute(values, ('dom', 'lon'), pairs)  13.3 us
    ppermute x4, starting transfers between devices, ring(): lax.ppermute(values, axis, [(i, (i + shift) % size) for i in range(size)])  3.82 us
    pallas_call x1, Pallas kernels, run_ends(): pl.pallas_call(ends_kernel, out_shape=jax.ShapeDtypeStruct(inner.shape, i...  2.99 us
    pallas_call x1, Pallas kernels, run_inner(): pl.pallas_call(inner_kernel, out_shape=(jax.ShapeDtypeStruct(fields.shape...  2.43 us
  transfers between devices with their start and end apart: 5, of which 2 were waited for; matrix products, arithmetic and copies ran while one was open for 0% of the time, Pallas kernels for 3%

profile of v5, /device:TPU:1, one launch (start us, length us, event | category | flops | bytes accessed | tf_op | source)
XLA Modules:
  0.0 88.7 jit_solution(10665196083618113859)
XLA Ops:
  0.0 0.0 copy-start.3
  0.0 3.2 %collective-permute-start.1 = (s32[1,2]{1,0:T(1,128)}, s32[1,2]{1,0:T(1,128)S(1)}, u32[]{:S(2)}, u32[]{:S(2)}) collective-permute-start(s32[1,2]{1,0:T(1,128)} %bitcast.11), channel_id=1, source_target_pairs={{0,3},{1,0},{2,1},{3,2},{4,7},{5,4},{6,5},{7,6},{8,11},{9,8},{10,9... | collective-permute-start | bytes 32 | tf_op jit(solution)/shard_map/ppermute | solution.py:406
  3.2 0.0 collective-permute-start
  3.2 0.0 copy-start
  3.2 1.2 %copy-done = f32[1,4,4,128,128]{4,3,2,1,0:T(8,128)S(1)} copy-done((f32[1,4,4,128,128]{4,3,2,1,0:T(8,128)S(1)}, f32[1,4,4,128,128]{4,3,2,1,0:T(8,128)}, u32[]{:S(2)}) %copy-start) | copy-done | bytes 1048600
  4.5 0.1 chunks.1.chunks_ref
  4.5 0.0 collective-permute-done.1.right_ref
  4.6 0.0 collective-permute-done.left_ref
  4.6 13.3 %collective-permute-start.2 = (s32[1,2]{1,0:T(1,128)S(1)}, s32[1,2]{1,0:T(1,128)S(1)}, u32[]{:S(2)}, u32[]{:S(2)}) collective-permute-start(s32[1,2]{1,0:T(1,128)S(1)} %collective-permute-done.left_ref), channel_id=1, source_target_pairs={{1,209},{3,211},{5,213},{7,215},{9,217},{11,219},{13,221},{15,223}... | collective-permute-start | bytes 32 | tf_op jit(solution)/shard_map/ppermute | solution.py:419
  17.8 0.9 %collective-permute-done.2.turn_ref = s32[1,2]{1,0:T(1,128)S(1)} collective-permute-done((s32[1,2]{1,0:T(1,128)S(1)}, s32[1,2]{1,0:T(1,128)S(1)}, u32[]{:S(2)}, u32[]{:S(2)}) %collective-permute-start.2) | collective-permute-done | bytes 40 | tf_op jit(solution)/shard_map/ppermute | solution.py:419
  18.8 0.0 copy-done.3
  18.8 0.1 table.1
  18.9 33.2 %all_to_all.10 = f32[64,33,1,128]{3,2,1,0:T(1,128)S(1)} all-to-all(f32[64,33,1,128]{3,2,1,0:T(1,128)S(1)} %bitcast.6), channel_id=1, replica_groups=mesh['dom'=64,'lon'=4] {'dom'}, dimensions={0} | all-to-all | bytes 2162688 | tf_op jit(solution)/shard_map/all_to_all | solution.py:431
  52.1 1.6 %blend.1 = f32[64,32,128]{2,1,0:T(8,128)S(1)} custom-call(f32[2112,128]{1,0:T(8,128)S(1)} %bitcast.9), custom_call_target="tpu_custom_call" | custom-call | flops 1081344 | bytes 2162688 | tf_op jit(solution)/shard_map/blend/pallas_call | solution.py:139
  53.7 0.0 copy-start.1
  53.7 0.0 copy-start.2
  53.7 27.8 %all_to_all.11 = f32[64,32,128]{2,1,0:T(8,128)S(1)} all-to-all(f32[64,32,128]{2,1,0:T(8,128)S(1)} %blend.1), channel_id=1, replica_groups=mesh['dom'=64,'lon'=4] {'dom'}, dimensions={0} | all-to-all | bytes 2097152 | tf_op jit(solution)/shard_map/all_to_all | solution.py:433
  81.5 0.0 copy-done.1
  81.5 0.0 copy-done.2
  81.5 0.4 pack.1
  81.9 0.1 collective-permute-start.3
  82.0 0.5 collective-permute-start.4
  82.5 2.4 %inner.1 = (f32[16,128,128]{2,1,0:T(8,128)S(1)}, f32[10,128,128]{2,1,0:T(8,128)S(1)}) custom-call(f32[16,128,128]{2,1,0:T(8,128)S(1)} %bitcast.8, f32[4,128,128]{2,1,0:T(8,128)S(1)} %copy-done.1, s32[128,128]{1,0:T(8,128)S(1)} %copy-done.2), custom_call_target="tpu_custom_call" | custom-call | flops 19660800 | bytes 3145728 | tf_op jit(solution)/shard_map/inner/pallas_call | solution.py:323
  84.9 0.0 collective-permute-done.3.before_ref
  84.9 0.8 collective-permute-done.4.after_ref
  85.8 3.0 %ends.1 = f32[16,128,128]{2,1,0:T(8,128)} custom-call(f32[16,128,128]{2,1,0:T(8,128)S(1)} %get-tuple-element.13.inner_ref, f32[10,128,128]{2,1,0:T(8,128)S(1)} %get-tuple-element.14.strip_ref, f32[128,128]{1,0:T(8,128)S(1)} %collective-permute-done.3.before_ref, f32[128,128]{1,0:T(8,128)S(1)} %collective-permute-done.4.after_ref), custom_call_target="tpu_custom_call" | custom-call | flops 10485760 | bytes 3145728 | tf_op jit(solution)/shard_map/ends/pallas_call | solution.py:387
Async XLA Ops:
  0.0 18.8 %copy-start.3 = (s32[1,2,1]{1,2,0:T(1,128)S(1)}, s32[1,2,1]{1,2,0:T(1,128)}, u32[]{:S(2)}) copy-start(s32[1,2,1]{1,2,0:T(1,128)} %param.7) | copy-start | bytes 28
  0.0 4.5 %collective-permute-start.1 = (s32[1,2]{1,0:T(1,128)}, s32[1,2]{1,0:T(1,128)S(1)}, u32[]{:S(2)}, u32[]{:S(2)}) collective-permute-start(s32[1,2]{1,0:T(1,128)} %bitcast.11), channel_id=1, source_target_pairs={{0,3},{1,0},{2,1},{3,2},{4,7},{5,4},{6,5},{7,6},{8,11},{9,8},{10,9... | collective-permute-start | bytes 32 | tf_op jit(solution)/shard_map/ppermute | solution.py:406
  3.2 1.3 %collective-permute-start = (s32[1,2]{1,0:T(1,128)}, s32[1,2]{1,0:T(1,128)S(1)}, u32[]{:S(2)}, u32[]{:S(2)}) collective-permute-start(s32[1,2]{1,0:T(1,128)} %bitcast.12), channel_id=1, source_target_pairs={{0,1},{1,2},{2,3},{3,0},{4,5},{5,6},{6,7},{7,4},{8,9},{9,10},{10,1... | collective-permute-start | bytes 32 | tf_op jit(solution)/shard_map/ppermute | solution.py:406
  3.2 1.2 %copy-start = (f32[1,4,4,128,128]{4,3,2,1,0:T(8,128)S(1)}, f32[1,4,4,128,128]{4,3,2,1,0:T(8,128)}, u32[]{:S(2)}) copy-start(f32[1,4,4,128,128]{4,3,2,1,0:T(8,128)} %param.4) | copy-start | bytes 3145732
  4.6 14.2 %collective-permute-start.2 = (s32[1,2]{1,0:T(1,128)S(1)}, s32[1,2]{1,0:T(1,128)S(1)}, u32[]{:S(2)}, u32[]{:S(2)}) collective-permute-start(s32[1,2]{1,0:T(1,128)S(1)} %collective-permute-done.left_ref), channel_id=1, source_target_pairs={{1,209},{3,211},{5,213},{7,215},{9,217},{11,219},{13,221},{15,223}... | collective-permute-start | bytes 32 | tf_op jit(solution)/shard_map/ppermute | solution.py:419
  53.7 27.8 %copy-start.1 = (f32[4,128,128]{2,1,0:T(8,128)S(1)}, f32[4,128,128]{2,1,0:T(8,128)}, u32[]{:S(2)}) copy-start(f32[4,128,128]{2,1,0:T(8,128)} %depth_ref.3) | copy-start | bytes 786436
  53.7 27.8 %copy-start.2 = (s32[128,128]{1,0:T(8,128)S(1)}, s32[128,128]{1,0:T(8,128)}, u32[]{:S(2)}) copy-start(s32[128,128]{1,0:T(8,128)} %levels_ref.3) | copy-start | bytes 196612
  81.9 3.0 %collective-permute-start.3 = (f32[128,128]{1,0:T(8,128)S(1)}, f32[128,128]{1,0:T(8,128)S(1)}, u32[]{:S(2)}, u32[]{:S(2)}) collective-permute-start(f32[128,128]{1,0:T(8,128)S(1)} %get-tuple-element.15), channel_id=1, source_target_pairs={{0,1},{1,2},{2,3},{3,0},{4,5},{5,6},{6,7},{7,4},{8,9},{9,10},{10,1... | collective-permute-start | bytes 196616 | tf_op jit(solution)/shard_map/ppermute | solution.py:406
  82.0 3.8 %collective-permute-start.4 = (f32[128,128]{1,0:T(8,128)S(1)}, f32[128,128]{1,0:T(8,128)S(1)}, u32[]{:S(2)}, u32[]{:S(2)}) collective-permute-start(f32[128,128]{1,0:T(8,128)S(1)} %get-tuple-element.16), channel_id=1, source_target_pairs={{0,3},{1,0},{2,1},{3,2},{4,7},{5,4},{6,5},{7,6},{8,11},{9,8},{10,9... | collective-permute-start | bytes 196616 | tf_op jit(solution)/shard_map/ppermute | solution.py:406

commit v6 on v5

--- a/solution.py
+++ b/solution.py
@@ -13,6 +13,7 @@
 LAT = 128
 WIDTH = 128
 HALO = 2 * STEPS
+PAIRS = ((0, 3), (1, 2))
 DOM = (2, 4, 8)
 HOP = (1, 2, 4)
 PAD = 8
@@ -159,8 +160,9 @@
 
 def groups():
     for kind in range(FIELDS + 1):
-        for level in range(LEV):
-            yield kind, level, kind * 2 + level % 2, level // 2
+        for which, pair in enumerate(PAIRS):
+            for half, level in enumerate(pair):
+                yield kind, level, kind * 2 + which, half
 
 
 def values_of(fields_ref, depth_ref, levels_ref, kind, level, start, rows):
@@ -280,15 +282,19 @@
     ]
 
 
-def couple_pairs(moved, wets):
-    even, odd = moved
-    within = exchange(even, odd, wets[0] & wets[1])
-    lane = lanes_of(LAT)
-    wet_even = jnp.where(wets[0], 1.0, 0.0)
-    turned = pltpu.roll(even, TILE, 1)
-    turned_wet = pltpu.roll(wet_even, TILE, 1) > 0.0
-    between = exchange(odd, turned, wets[1] & turned_wet & (lane < TILE))
-    return [even + within - pltpu.roll(between, TILE, 1), odd + between - within]
+def couple_pairs():
+    known = []
+
+    def couple(moved, wets):
+        outer, middle = moved
+        if not known:
+            turned_wet = pltpu.roll(jnp.where(wets[1], 1.0, 0.0), TILE, 1) > 0.0
+            known.append(jnp.where(wets[1] & turned_wet, vertical_mix, 0.0))
+        across = exchange(outer, middle, wets[0] & wets[1])
+        between = known[0] * (pltpu.roll(middle, TILE, 1) - middle)
+        return [outer + across, middle + between - across]
+
+    return couple
 
 
 def scratch_for(count):
@@ -299,17 +305,27 @@
 PROWS = 128
 
 
+def ring_base(half):
+    return (WIDTH - STRIP + TILE * half) % WIDTH
+
+
+def turned(values, shift):
+    return pltpu.roll(values, shift % WIDTH, 1) if shift % WIDTH else values
+
+
 def inner_kernel(fields_ref, depth_ref, levels_ref, out_ref, strip_ref, *scratch):
     lane = lanes_of(LAT)
+    place = (lane + (WIDTH - ring_base(0))) % TILE
+    second = (lane >= ring_base(1)) & (lane < ring_base(0))
     for kind, level, slot, half in groups():
         values = values_of(fields_ref, depth_ref, levels_ref, kind, level, 0, LAT)
         scratch[kind][level, PAD : PAD + LAT, :] = values
-        base = half * TILE
+        base = ring_base(half)
         ends = jnp.where(
-            lane < base + 24, pltpu.roll(values, base + STRIP, 1), pltpu.roll(values, base + 2 * STRIP, 1)
+            place < 2 * STRIP, turned(values, base - (WIDTH - STRIP)), turned(values, base + 2 * STRIP)
         )
         if half:
-            strip_ref[slot] = jnp.where(lane < TILE, strip_ref[slot], ends)
+            strip_ref[slot] = jnp.where(second, ends, strip_ref[slot])
         else:
             strip_ref[slot] = ends
 
@@ -337,7 +353,7 @@
 
 def ends_kernel(inner_ref, strip_ref, before_ref, after_ref, out_ref, result_ref, sems, *scratch):
     lane = lanes_of(LAT)
-    place = lane % TILE
+    place = (lane + (WIDTH - ring_base(0))) % TILE
     in_after = (place >= STRIP) & (place < STRIP + HALO)
     in_before = (place >= STRIP + HALO) & (place < 2 * STRIP)
     before = before_ref[...]
@@ -348,19 +364,19 @@
             low = HALO * slot
             values = jnp.where(
                 in_after,
-                pltpu.roll(after, (WIDTH + STRIP - low - HALO) % WIDTH, 1),
+                turned(after, ring_base(0) + STRIP - low - HALO),
                 jnp.where(
-                    in_before, pltpu.roll(before, (WIDTH + STRIP + HALO - low) % WIDTH, 1), strip_ref[slot]
+                    in_before, turned(before, ring_base(0) + STRIP + HALO - low), strip_ref[slot]
                 ),
             )
             scratch[kind][which, PAD : PAD + LAT, :] = values
 
     def emit(kind, which, values):
         for half in range(2):
-            base = half * TILE
-            at = kind * LEV + which + 2 * half
-            last_columns = pltpu.roll(values, (WIDTH - STRIP - base) % WIDTH, 1)
-            first_columns = pltpu.roll(values, (2 * WIDTH - base - 2 * STRIP) % WIDTH, 1)
+            base = ring_base(half)
+            at = kind * LEV + PAIRS[which][half]
+            last_columns = turned(values, WIDTH - STRIP - base)
+            first_columns = turned(values, -(base + 2 * STRIP))
             result_ref[at] = jnp.where(
                 lane < HALO, first_columns, jnp.where(lane >= WIDTH - HALO, last_columns, inner_ref[at])
             )
@@ -376,7 +392,7 @@
         copies[1].start()
         copies[2].start()
 
-    march(scratch, 2, couple_pairs, emit, winds_done)
+    march(scratch, 2, couple_pairs(), emit, winds_done)
     copies[0].start()
     copies[3].start()
     for copy in copies:

time: 89 us -> 88.6 us (level)
  no operation moved by 1% of the time
where the time goes in v6:
time: 88.6 us; the launch traced here: 88.4 us
  blocking collectives  61 us (69%)
  starting transfers between devices  17.1 us (19%)
  Pallas kernels  7.05 us (8%)
  waiting for transfers between devices  1.91 us (2%)
  local copies, waits for them, and re-layouts  1.24 us (1%)
    all_to_all x1, blocking collectives, on_device(): block = lax.all_to_all(sent, 'dom', split_axis=0, concat_axis=0, tiled=True)  33.2 us
    all_to_all x1, blocking collectives, on_device(): back = lax.all_to_all(mixed, 'dom', split_axis=0, concat_axis=0, tiled=True)  27.8 us
    ppermute x1, starting transfers between devices, take_turns(): return lax.ppermute(values, ('dom', 'lon'), pairs)  13.3 us
    ppermute x4, starting transfers between devices, ring(): lax.ppermute(values, axis, [(i, (i + shift) % size) for i in range(size)])  3.82 us
    pallas_call x1, Pallas kernels, run_ends(): pl.pallas_call(ends_kernel, out_shape=jax.ShapeDtypeStruct(inner.shape, i...  2.66 us
    pallas_call x1, Pallas kernels, run_inner(): pl.pallas_call(inner_kernel, out_shape=(jax.ShapeDtypeStruct(fields.shape...  2.27 us
  transfers between devices with their start and end apart: 5, of which 2 were waited for; matrix products, arithmetic and copies ran while one was open for 0% of the time, Pallas kernels for 3%

profile of v6, /device:TPU:1, one launch (start us, length us, event | category | flops | bytes accessed | tf_op | source)
XLA Modules:
  0.0 88.4 jit_solution(4837188429014652003)
XLA Ops:
  0.0 0.0 copy-start.3
  0.0 3.2 %collective-permute-start.1 = (s32[1,2]{1,0:T(1,128)}, s32[1,2]{1,0:T(1,128)S(1)}, u32[]{:S(2)}, u32[]{:S(2)}) collective-permute-start(s32[1,2]{1,0:T(1,128)} %bitcast.11), channel_id=1, source_target_pairs={{0,3},{1,0},{2,1},{3,2},{4,7},{5,4},{6,5},{7,6},{8,11},{9,8},{10,9... | collective-permute-start | bytes 32 | tf_op jit(solution)/shard_map/ppermute | solution.py:422
  3.2 0.0 collective-permute-start
  3.2 0.0 copy-start
  3.2 1.2 %copy-done = f32[1,4,4,128,128]{4,3,2,1,0:T(8,128)S(1)} copy-done((f32[1,4,4,128,128]{4,3,2,1,0:T(8,128)S(1)}, f32[1,4,4,128,128]{4,3,2,1,0:T(8,128)}, u32[]{:S(2)}) %copy-start) | copy-done | bytes 1048600
  4.5 0.1 chunks.1.chunks_ref
  4.5 0.0 collective-permute-done.1.right_ref
  4.6 0.0 collective-permute-done.left_ref
  4.6 13.3 %collective-permute-start.2 = (s32[1,2]{1,0:T(1,128)S(1)}, s32[1,2]{1,0:T(1,128)S(1)}, u32[]{:S(2)}, u32[]{:S(2)}) collective-permute-start(s32[1,2]{1,0:T(1,128)S(1)} %collective-permute-done.left_ref), channel_id=1, source_target_pairs={{1,209},{3,211},{5,213},{7,215},{9,217},{11,219},{13,221},{15,223}... | collective-permute-start | bytes 32 | tf_op jit(solution)/shard_map/ppermute | solution.py:435
  17.8 0.9 %collective-permute-done.2.turn_ref = s32[1,2]{1,0:T(1,128)S(1)} collective-permute-done((s32[1,2]{1,0:T(1,128)S(1)}, s32[1,2]{1,0:T(1,128)S(1)}, u32[]{:S(2)}, u32[]{:S(2)}) %collective-permute-start.2) | collective-permute-done | bytes 40 | tf_op jit(solution)/shard_map/ppermute | solution.py:435
  18.8 0.0 copy-done.3
  18.8 0.1 table.1
  18.9 33.2 %all_to_all.10 = f32[64,33,1,128]{3,2,1,0:T(1,128)S(1)} all-to-all(f32[64,33,1,128]{3,2,1,0:T(1,128)S(1)} %bitcast.6), channel_id=1, replica_groups=mesh['dom'=64,'lon'=4] {'dom'}, dimensions={0} | all-to-all | bytes 2162688 | tf_op jit(solution)/shard_map/all_to_all | solution.py:447
  52.1 1.6 %blend.1 = f32[64,32,128]{2,1,0:T(8,128)S(1)} custom-call(f32[2112,128]{1,0:T(8,128)S(1)} %bitcast.9), custom_call_target="tpu_custom_call" | custom-call | flops 1081344 | bytes 2162688 | tf_op jit(solution)/shard_map/blend/pallas_call | solution.py:140
  53.7 0.0 copy-start.1
  53.7 0.0 copy-start.2
  53.7 27.8 %all_to_all.11 = f32[64,32,128]{2,1,0:T(8,128)S(1)} all-to-all(f32[64,32,128]{2,1,0:T(8,128)S(1)} %blend.1), channel_id=1, replica_groups=mesh['dom'=64,'lon'=4] {'dom'}, dimensions={0} | all-to-all | bytes 2097152 | tf_op jit(solution)/shard_map/all_to_all | solution.py:449
  81.5 0.0 copy-done.1
  81.5 0.0 copy-done.2
  81.5 0.4 pack.1
  81.9 0.1 collective-permute-start.3
  82.0 0.5 collective-permute-start.4
  82.5 2.3 %inner.1 = (f32[16,128,128]{2,1,0:T(8,128)S(1)}, f32[10,128,128]{2,1,0:T(8,128)S(1)}) custom-call(f32[16,128,128]{2,1,0:T(8,128)S(1)} %bitcast.8, f32[4,128,128]{2,1,0:T(8,128)S(1)} %copy-done.1, s32[128,128]{1,0:T(8,128)S(1)} %copy-done.2), custom_call_target="tpu_custom_call" | custom-call | flops 19660800 | bytes 3145728 | tf_op jit(solution)/shard_map/inner/pallas_call | solution.py:339
  84.8 0.0 collective-permute-done.3.before_ref
  84.8 1.0 %collective-permute-done.4.after_ref = f32[128,128]{1,0:T(8,128)S(1)} collective-permute-done((f32[128,128]{1,0:T(8,128)S(1)}, f32[128,128]{1,0:T(8,128)S(1)}, u32[]{:S(2)}, u32[]{:S(2)}) %collective-permute-start.4) | collective-permute-done | bytes 65568 | tf_op jit(solution)/shard_map/ppermute | solution.py:422
  85.8 2.7 %ends.1 = f32[16,128,128]{2,1,0:T(8,128)} custom-call(f32[16,128,128]{2,1,0:T(8,128)S(1)} %get-tuple-element.13.inner_ref, f32[10,128,128]{2,1,0:T(8,128)S(1)} %get-tuple-element.14.strip_ref, f32[128,128]{1,0:T(8,128)S(1)} %collective-permute-done.3.before_ref, f32[128,128]{1,0:T(8,128)S(1)} %collective-permute-done.4.after_ref), custom_call_target="tpu_custom_call" | custom-call | flops 10485760 | bytes 3145728 | tf_op jit(solution)/shard_map/ends/pallas_call | solution.py:403
Async XLA Ops:
  0.0 18.8 %copy-start.3 = (s32[1,2,1]{1,2,0:T(1,128)S(1)}, s32[1,2,1]{1,2,0:T(1,128)}, u32[]{:S(2)}) copy-start(s32[1,2,1]{1,2,0:T(1,128)} %param.7) | copy-start | bytes 28
  0.0 4.5 %collective-permute-start.1 = (s32[1,2]{1,0:T(1,128)}, s32[1,2]{1,0:T(1,128)S(1)}, u32[]{:S(2)}, u32[]{:S(2)}) collective-permute-start(s32[1,2]{1,0:T(1,128)} %bitcast.11), channel_id=1, source_target_pairs={{0,3},{1,0},{2,1},{3,2},{4,7},{5,4},{6,5},{7,6},{8,11},{9,8},{10,9... | collective-permute-start | bytes 32 | tf_op jit(solution)/shard_map/ppermute | solution.py:422
  3.2 1.3 %collective-permute-start = (s32[1,2]{1,0:T(1,128)}, s32[1,2]{1,0:T(1,128)S(1)}, u32[]{:S(2)}, u32[]{:S(2)}) collective-permute-start(s32[1,2]{1,0:T(1,128)} %bitcast.12), channel_id=1, source_target_pairs={{0,1},{1,2},{2,3},{3,0},{4,5},{5,6},{6,7},{7,4},{8,9},{9,10},{10,1... | collective-permute-start | bytes 32 | tf_op jit(solution)/shard_map/ppermute | solution.py:422
  3.2 1.2 %copy-start = (f32[1,4,4,128,128]{4,3,2,1,0:T(8,128)S(1)}, f32[1,4,4,128,128]{4,3,2,1,0:T(8,128)}, u32[]{:S(2)}) copy-start(f32[1,4,4,128,128]{4,3,2,1,0:T(8,128)} %param.4) | copy-start | bytes 3145732
  4.6 14.2 %collective-permute-start.2 = (s32[1,2]{1,0:T(1,128)S(1)}, s32[1,2]{1,0:T(1,128)S(1)}, u32[]{:S(2)}, u32[]{:S(2)}) collective-permute-start(s32[1,2]{1,0:T(1,128)S(1)} %collective-permute-done.left_ref), channel_id=1, source_target_pairs={{1,209},{3,211},{5,213},{7,215},{9,217},{11,219},{13,221},{15,223}... | collective-permute-start | bytes 32 | tf_op jit(solution)/shard_map/ppermute | solution.py:435
  53.7 27.8 %copy-start.1 = (f32[4,128,128]{2,1,0:T(8,128)S(1)}, f32[4,128,128]{2,1,0:T(8,128)}, u32[]{:S(2)}) copy-start(f32[4,128,128]{2,1,0:T(8,128)} %depth_ref.3) | copy-start | bytes 786436
  53.7 27.8 %copy-start.2 = (s32[128,128]{1,0:T(8,128)S(1)}, s32[128,128]{1,0:T(8,128)}, u32[]{:S(2)}) copy-start(s32[128,128]{1,0:T(8,128)} %levels_ref.3) | copy-start | bytes 196612
  81.9 2.9 %collective-permute-start.3 = (f32[128,128]{1,0:T(8,128)S(1)}, f32[128,128]{1,0:T(8,128)S(1)}, u32[]{:S(2)}, u32[]{:S(2)}) collective-permute-start(f32[128,128]{1,0:T(8,128)S(1)} %get-tuple-element.15), channel_id=1, source_target_pairs={{0,1},{1,2},{2,3},{3,0},{4,5},{5,6},{6,7},{7,4},{8,9},{9,10},{10,1... | collective-permute-start | bytes 196616 | tf_op jit(solution)/shard_map/ppermute | solution.py:422
  82.0 3.8 %collective-permute-start.4 = (f32[128,128]{1,0:T(8,128)S(1)}, f32[128,128]{1,0:T(8,128)S(1)}, u32[]{:S(2)}, u32[]{:S(2)}) collective-permute-start(f32[128,128]{1,0:T(8,128)S(1)} %get-tuple-element.16), channel_id=1, source_target_pairs={{0,3},{1,0},{2,1},{3,2},{4,7},{5,4},{6,5},{7,6},{8,11},{9,8},{10,9... | collective-permute-start | bytes 196616 | tf_op jit(solution)/shard_map/ppermute | solution.py:422

commit v7 on v6

--- a/solution.py
+++ b/solution.py
@@ -88,7 +88,7 @@
 SHARE = WIDTH // 4
 TOGETHER = 8
 BROWS = 32
-UNROLL = 2
+UNROLL = 8
 
 
 def blend_kernel(block_ref, out_ref, numbers_ref, table_ref, sem):
@@ -203,7 +203,7 @@
     )(fields, depth, levels)
 
 
-def march(scratch, count, couple, emit, winds_done=lambda: None):
+def march(scratch, count, couple, emit):
     height, zonal, merid, tracer, thick, flux, south, north = scratch
 
     def rows_at(ref, shift):
@@ -247,7 +247,6 @@
             for which in range(count):
                 emit(1, which, new_u[which])
                 emit(2, which, new_v[which])
-            winds_done()
         else:
             put(zonal, new_u)
             put(merid, new_v)
@@ -256,12 +255,14 @@
         dy = rows_at(flux, 1) - rows_at(flux, -1)
         new_h = jnp.where(wet, part - half * dy, 0.0)
         new_c = jnp.where(wet, c_part + (rows_at(south, 1) + rows_at(north, -1)), 0.0)
+        if last:
+            for which in range(count):
+                emit(0, which, new_h[which])
         moved = [new_c[which] for which in range(count)]
         wets = [wet[which] for which in range(count)]
         coupled = couple(moved, wets)
         for which in range(count):
             if last:
-                emit(0, which, new_h[which])
                 emit(3, which, coupled[which])
             else:
                 height[which, PAD : PAD + LAT, :] = new_h[which]
@@ -371,6 +372,8 @@
             )
             scratch[kind][which, PAD : PAD + LAT, :] = values
 
+    copies = []
+
     def emit(kind, which, values):
         for half in range(2):
             base = ring_base(half)
@@ -380,21 +383,10 @@
             result_ref[at] = jnp.where(
                 lane < HALO, first_columns, jnp.where(lane >= WIDTH - HALO, last_columns, inner_ref[at])
             )
-
-    copies = [
-        pltpu.make_async_copy(
-            result_ref.at[kind * LEV : kind * LEV + LEV], out_ref.at[kind * LEV : kind * LEV + LEV], sems.at[kind]
-        )
-        for kind in range(FIELDS)
-    ]
-
-    def winds_done():
-        copies[1].start()
-        copies[2].start()
-
-    march(scratch, 2, couple_pairs(), emit, winds_done)
-    copies[0].start()
-    copies[3].start()
+            copies.append(pltpu.make_async_copy(result_ref.at[at], out_ref.at[at], sems.at[at]))
+            copies[-1].start()
+
+    march(scratch, 2, couple_pairs(), emit)
     for copy in copies:
         copy.wait()
 
@@ -405,7 +397,7 @@
         out_shape=jax.ShapeDtypeStruct(inner.shape, inner.dtype),
         in_specs=vmem(4),
         out_specs=pl.BlockSpec(memory_space=pl.ANY),
-        scratch_shapes=[pltpu.VMEM(inner.shape, inner.dtype), pltpu.SemaphoreType.DMA((FIELDS,))] + scratch_for(2),
+        scratch_shapes=[pltpu.VMEM(inner.shape, inner.dtype), pltpu.SemaphoreType.DMA((FIELDS * LEV,))] + scratch_for(2),
         compiler_params=pltpu.CompilerParams(vmem_limit_bytes=VMEM_LIMIT),
         cost_estimate=pl.CostEstimate(flops=40 * inner.size, bytes_accessed=12 * inner.size, transcendentals=0),
         name="ends",

time: 88.6 us -> 87.9 us (level)
  no operation moved by 1% of the time
where the time goes in v7:
time: 87.9 us; the launch traced here: 87.7 us
  blocking collectives  61 us (69%)
  starting transfers between devices  17.1 us (19%)
  Pallas kernels  6.34 us (7%)
  waiting for transfers between devices  1.91 us (2%)
  local copies, waits for them, and re-layouts  1.24 us (1%)
    all_to_all x1, blocking collectives, on_device(): block = lax.all_to_all(sent, 'dom', split_axis=0, concat_axis=0, tiled=True)  33.2 us
    all_to_all x1, blocking collectives, on_device(): back = lax.all_to_all(mixed, 'dom', split_axis=0, concat_axis=0, tiled=True)  27.8 us
    ppermute x1, starting transfers between devices, take_turns(): return lax.ppermute(values, ('dom', 'lon'), pairs)  13.3 us
    ppermute x4, starting transfers between devices, ring(): lax.ppermute(values, axis, [(i, (i + shift) % size) for i in range(size)])  3.82 us
    pallas_call x1, Pallas kernels, run_ends(): pl.pallas_call(ends_kernel, out_shape=jax.ShapeDtypeStruct(inner.shape, i...  2.57 us
    pallas_call x1, Pallas kernels, run_inner(): pl.pallas_call(inner_kernel, out_shape=(jax.ShapeDtypeStruct(fields.shape...  2.27 us
  transfers between devices with their start and end apart: 5, of which 2 were waited for; matrix products, arithmetic and copies ran while one was open for 0% of the time, Pallas kernels for 3%

profile of v7, /device:TPU:1, one launch (start us, length us, event | category | flops | bytes accessed | tf_op | source)
XLA Modules:
  0.0 87.7 jit_solution(6790013863746339228)
XLA Ops:
  0.0 0.0 copy-start.3
  0.0 3.2 %collective-permute-start.1 = (s32[1,2]{1,0:T(1,128)}, s32[1,2]{1,0:T(1,128)S(1)}, u32[]{:S(2)}, u32[]{:S(2)}) collective-permute-start(s32[1,2]{1,0:T(1,128)} %bitcast.11), channel_id=1, source_target_pairs={{0,3},{1,0},{2,1},{3,2},{4,7},{5,4},{6,5},{7,6},{8,11},{9,8},{10,9... | collective-permute-start | bytes 32 | tf_op jit(solution)/shard_map/ppermute | solution.py:414
  3.2 0.0 collective-permute-start
  3.2 0.0 copy-start
  3.2 1.2 %copy-done = f32[1,4,4,128,128]{4,3,2,1,0:T(8,128)S(1)} copy-done((f32[1,4,4,128,128]{4,3,2,1,0:T(8,128)S(1)}, f32[1,4,4,128,128]{4,3,2,1,0:T(8,128)}, u32[]{:S(2)}) %copy-start) | copy-done | bytes 1048600
  4.5 0.1 chunks.1.chunks_ref
  4.5 0.0 collective-permute-done.1.right_ref
  4.6 0.0 collective-permute-done.left_ref
  4.6 13.3 %collective-permute-start.2 = (s32[1,2]{1,0:T(1,128)S(1)}, s32[1,2]{1,0:T(1,128)S(1)}, u32[]{:S(2)}, u32[]{:S(2)}) collective-permute-start(s32[1,2]{1,0:T(1,128)S(1)} %collective-permute-done.left_ref), channel_id=1, source_target_pairs={{1,209},{3,211},{5,213},{7,215},{9,217},{11,219},{13,221},{15,223}... | collective-permute-start | bytes 32 | tf_op jit(solution)/shard_map/ppermute | solution.py:427
  17.8 0.9 %collective-permute-done.2.turn_ref = s32[1,2]{1,0:T(1,128)S(1)} collective-permute-done((s32[1,2]{1,0:T(1,128)S(1)}, s32[1,2]{1,0:T(1,128)S(1)}, u32[]{:S(2)}, u32[]{:S(2)}) %collective-permute-start.2) | collective-permute-done | bytes 40 | tf_op jit(solution)/shard_map/ppermute | solution.py:427
  18.8 0.0 copy-done.3
  18.8 0.1 table.1
  18.9 33.2 %all_to_all.10 = f32[64,33,1,128]{3,2,1,0:T(1,128)S(1)} all-to-all(f32[64,33,1,128]{3,2,1,0:T(1,128)S(1)} %bitcast.6), channel_id=1, replica_groups=mesh['dom'=64,'lon'=4] {'dom'}, dimensions={0} | all-to-all | bytes 2162688 | tf_op jit(solution)/shard_map/all_to_all | solution.py:439
  52.1 0.9 %blend.1 = f32[64,32,128]{2,1,0:T(8,128)S(1)} custom-call(f32[2112,128]{1,0:T(8,128)S(1)} %bitcast.9), custom_call_target="tpu_custom_call" | custom-call | flops 1081344 | bytes 2162688 | tf_op jit(solution)/shard_map/blend/pallas_call | solution.py:140
  53.0 0.0 copy-start.1
  53.0 0.0 copy-start.2
  53.1 27.8 %all_to_all.11 = f32[64,32,128]{2,1,0:T(8,128)S(1)} all-to-all(f32[64,32,128]{2,1,0:T(8,128)S(1)} %blend.1), channel_id=1, replica_groups=mesh['dom'=64,'lon'=4] {'dom'}, dimensions={0} | all-to-all | bytes 2097152 | tf_op jit(solution)/shard_map/all_to_all | solution.py:441
  80.9 0.0 copy-done.1
  80.9 0.0 copy-done.2
  80.9 0.4 pack.1
  81.3 0.1 collective-permute-start.3
  81.4 0.5 collective-permute-start.4
  81.9 2.3 %inner.1 = (f32[16,128,128]{2,1,0:T(8,128)S(1)}, f32[10,128,128]{2,1,0:T(8,128)S(1)}) custom-call(f32[16,128,128]{2,1,0:T(8,128)S(1)} %bitcast.8, f32[4,128,128]{2,1,0:T(8,128)S(1)} %copy-done.1, s32[128,128]{1,0:T(8,128)S(1)} %copy-done.2), custom_call_target="tpu_custom_call" | custom-call | flops 19660800 | bytes 3145728 | tf_op jit(solution)/shard_map/inner/pallas_call | solution.py:340
  84.1 0.0 collective-permute-done.3.before_ref
  84.2 1.0 %collective-permute-done.4.after_ref = f32[128,128]{1,0:T(8,128)S(1)} collective-permute-done((f32[128,128]{1,0:T(8,128)S(1)}, f32[128,128]{1,0:T(8,128)S(1)}, u32[]{:S(2)}, u32[]{:S(2)}) %collective-permute-start.4) | collective-permute-done | bytes 65568 | tf_op jit(solution)/shard_map/ppermute | solution.py:414
  85.1 2.6 %ends.1 = f32[16,128,128]{2,1,0:T(8,128)} custom-call(f32[16,128,128]{2,1,0:T(8,128)S(1)} %get-tuple-element.13.inner_ref, f32[10,128,128]{2,1,0:T(8,128)S(1)} %get-tuple-element.14.strip_ref, f32[128,128]{1,0:T(8,128)S(1)} %collective-permute-done.3.before_ref, f32[128,128]{1,0:T(8,128)S(1)} %collective-permute-done.4.after_ref), custom_call_target="tpu_custom_call" | custom-call | flops 10485760 | bytes 3145728 | tf_op jit(solution)/shard_map/ends/pallas_call | solution.py:395
Async XLA Ops:
  0.0 18.8 %copy-start.3 = (s32[1,2,1]{1,2,0:T(1,128)S(1)}, s32[1,2,1]{1,2,0:T(1,128)}, u32[]{:S(2)}) copy-start(s32[1,2,1]{1,2,0:T(1,128)} %param.7) | copy-start | bytes 28
  0.0 4.5 %collective-permute-start.1 = (s32[1,2]{1,0:T(1,128)}, s32[1,2]{1,0:T(1,128)S(1)}, u32[]{:S(2)}, u32[]{:S(2)}) collective-permute-start(s32[1,2]{1,0:T(1,128)} %bitcast.11), channel_id=1, source_target_pairs={{0,3},{1,0},{2,1},{3,2},{4,7},{5,4},{6,5},{7,6},{8,11},{9,8},{10,9... | collective-permute-start | bytes 32 | tf_op jit(solution)/shard_map/ppermute | solution.py:414
  3.2 1.3 %collective-permute-start = (s32[1,2]{1,0:T(1,128)}, s32[1,2]{1,0:T(1,128)S(1)}, u32[]{:S(2)}, u32[]{:S(2)}) collective-permute-start(s32[1,2]{1,0:T(1,128)} %bitcast.12), channel_id=1, source_target_pairs={{0,1},{1,2},{2,3},{3,0},{4,5},{5,6},{6,7},{7,4},{8,9},{9,10},{10,1... | collective-permute-start | bytes 32 | tf_op jit(solution)/shard_map/ppermute | solution.py:414
  3.2 1.2 %copy-start = (f32[1,4,4,128,128]{4,3,2,1,0:T(8,128)S(1)}, f32[1,4,4,128,128]{4,3,2,1,0:T(8,128)}, u32[]{:S(2)}) copy-start(f32[1,4,4,128,128]{4,3,2,1,0:T(8,128)} %param.4) | copy-start | bytes 3145732
  4.6 14.2 %collective-permute-start.2 = (s32[1,2]{1,0:T(1,128)S(1)}, s32[1,2]{1,0:T(1,128)S(1)}, u32[]{:S(2)}, u32[]{:S(2)}) collective-permute-start(s32[1,2]{1,0:T(1,128)S(1)} %collective-permute-done.left_ref), channel_id=1, source_target_pairs={{1,209},{3,211},{5,213},{7,215},{9,217},{11,219},{13,221},{15,223}... | collective-permute-start | bytes 32 | tf_op jit(solution)/shard_map/ppermute | solution.py:427
  53.0 27.8 %copy-start.1 = (f32[4,128,128]{2,1,0:T(8,128)S(1)}, f32[4,128,128]{2,1,0:T(8,128)}, u32[]{:S(2)}) copy-start(f32[4,128,128]{2,1,0:T(8,128)} %depth_ref.3) | copy-start | bytes 786436
  53.0 27.8 %copy-start.2 = (s32[128,128]{1,0:T(8,128)S(1)}, s32[128,128]{1,0:T(8,128)}, u32[]{:S(2)}) copy-start(s32[128,128]{1,0:T(8,128)} %levels_ref.3) | copy-start | bytes 196612
  81.3 2.9 %collective-permute-start.3 = (f32[128,128]{1,0:T(8,128)S(1)}, f32[128,128]{1,0:T(8,128)S(1)}, u32[]{:S(2)}, u32[]{:S(2)}) collective-permute-start(f32[128,128]{1,0:T(8,128)S(1)} %get-tuple-element.15), channel_id=1, source_target_pairs={{0,1},{1,2},{2,3},{3,0},{4,5},{5,6},{6,7},{7,4},{8,9},{9,10},{10,1... | collective-permute-start | bytes 196616 | tf_op jit(solution)/shard_map/ppermute | solution.py:414
  81.4 3.8 %collective-permute-start.4 = (f32[128,128]{1,0:T(8,128)S(1)}, f32[128,128]{1,0:T(8,128)S(1)}, u32[]{:S(2)}, u32[]{:S(2)}) collective-permute-start(f32[128,128]{1,0:T(8,128)S(1)} %get-tuple-element.16), channel_id=1, source_target_pairs={{0,3},{1,0},{2,1},{3,2},{4,7},{5,4},{6,5},{7,6},{8,11},{9,8},{10,9... | collective-permute-start | bytes 196616 | tf_op jit(solution)/shard_map/ppermute | solution.py:414

commit v8 on v7

--- a/solution.py
+++ b/solution.py
@@ -61,7 +61,7 @@
 def add_table(chunks, own, left, right, turn, count):
     height = chunks.shape[0] // count
 
-    def table_kernel(own_ref, left_ref, right_ref, turn_ref, chunks_ref, out_ref):
+    def table_kernel(turn_ref, own_ref, left_ref, right_ref, chunks_ref, out_ref):
         del turn_ref, chunks_ref
         tile = lanes_of(1) % 4
         picks = (left_ref[0:1, 1:2], own_ref[0:1, 0:1], own_ref[0:1, 1:2], right_ref[0:1, 0:1])
@@ -82,7 +82,7 @@
         compiler_params=pltpu.CompilerParams(vmem_limit_bytes=VMEM_LIMIT),
         cost_estimate=pl.CostEstimate(flops=0, bytes_accessed=4 * count * WIDTH, transcendentals=0),
         name="table",
-    )(own, left, right, turn, chunks)
+    )(turn, own, left, right, chunks)
 
 
 SHARE = WIDTH // 4
@@ -424,17 +424,18 @@
         there = there * columns + (column + HOP[1]) % columns
         there = there * layers + (layer + HOP[2]) % layers
         pairs += [(here * bands + band, there * bands + band) for band in range(1, bands, 2)]
-    return lax.ppermute(values, ("dom", "lon"), pairs)
+    values = lax.ppermute(values, ("dom", "lon"), pairs)
+    return lax.ppermute(values, "lon", [(1, 3), (3, 1)])
 
 
 def on_device(state, level_thickness, wet_levels, ancestors):
     size = lax.axis_size("dom")
     own = ancestors.reshape(1, -1)
+    turn = take_turns(own)
     left = ring(own, "lon", 1)
     right = ring(own, "lon", -1)
     chunks = make_chunks(state.reshape(size, -1, WIDTH))
-    left, right = lax.optimization_barrier((left, right))
-    chunks = add_table(chunks, own, left, right, take_turns(left), size)
+    chunks = add_table(chunks, own, left, right, turn, size)
     sent = chunks.reshape(size, -1, 1, WIDTH)
     block = lax.all_to_all(sent, "dom", split_axis=0, concat_axis=0, tiled=True)
     mixed = blend(block.reshape(chunks.shape), size)

time: 87.9 us -> 87.6 us (level)
  blocking collectives: 61 us -> 57.4 us
  starting transfers between devices: 17.1 us -> 19.4 us
  waiting for transfers between devices: 1.91 us -> 2.95 us
    ppermute x1 -> x2, starting transfers between devices: 13.3 us -> 15.5 us  [the longest x1 13.2 us: take_turns(): values = lax.ppermute(values, ('dom', 'lon'), pairs)]
    all_to_all x1, blocking collectives: 27.8 us -> 25.7 us  [on_device(): back = lax.all_to_all(mixed, 'dom', split_axis=0, concat_axis=0, tiled=True)]
    all_to_all x1, blocking collectives: 33.2 us -> 31.7 us  [on_device(): block = lax.all_to_all(sent, 'dom', split_axis=0, concat_axis=0, tiled=True)]
    ppermute x1 -> x2, waiting for transfers between devices: 0.91 us -> 1.95 us  [the longest x1 1.95 us: take_turns(): return lax.ppermute(values, 'lon', [(1, 3), (3, 1)])]
  transfers between devices with their start and end apart: 5 -> 6, of which waited for: 2 -> 2; matrix products, arithmetic and copies ran while one was open for 0% -> 0% of each run, Pallas kernels for 3% -> 3%
where the time goes in v8:
time: 87.6 us; the launch traced here: 87.4 us
  blocking collectives  57.4 us (66%)
  starting transfers between devices  19.4 us (22%)
  Pallas kernels  6.35 us (7%)
  waiting for transfers between devices  2.95 us (3%)
  local copies, waits for them, and re-layouts  1.23 us (1%)
    all_to_all x1, blocking collectives, on_device(): block = lax.all_to_all(sent, 'dom', split_axis=0, concat_axis=0, tiled=True)  31.7 us
    all_to_all x1, blocking collectives, on_device(): back = lax.all_to_all(mixed, 'dom', split_axis=0, concat_axis=0, tiled=True)  25.7 us
    ppermute x1, starting transfers between devices, take_turns(): values = lax.ppermute(values, ('dom', 'lon'), pairs)  13.2 us
    ppermute x4, starting transfers between devices, ring(): lax.ppermute(values, axis, [(i, (i + shift) % size) for i in range(size)])  3.82 us
    pallas_call x1, Pallas kernels, run_ends(): pl.pallas_call(ends_kernel, out_shape=jax.ShapeDtypeStruct(inner.shape, i...  2.57 us
    ppermute x1, starting transfers between devices, take_turns(): return lax.ppermute(values, 'lon', [(1, 3), (3, 1)])  2.31 us
    pallas_call x1, Pallas kernels, run_inner(): pl.pallas_call(inner_kernel, out_shape=(jax.ShapeDtypeStruct(fields.shape...  2.27 us
    ppermute x1, waiting for transfers between devices, take_turns(): return lax.ppermute(values, 'lon', [(1, 3), (3, 1)])  1.95 us
  transfers between devices with their start and end apart: 6, of which 2 were waited for; matrix products, arithmetic and copies ran while one was open for 0% of the time, Pallas kernels for 3%

profile of v8, /device:TPU:1, one launch (start us, length us, event | category | flops | bytes accessed | tf_op | source)
XLA Modules:
  0.0 87.4 jit_solution(12092975620663182993)
XLA Ops:
  0.0 0.0 copy-start.3
  0.0 3.2 %collective-permute-start.3 = (s32[1,2]{1,0:T(1,128)}, s32[1,2]{1,0:T(1,128)S(1)}, u32[]{:S(2)}, u32[]{:S(2)}) collective-permute-start(s32[1,2]{1,0:T(1,128)} %bitcast.11), channel_id=1, source_target_pairs={{0,3},{1,0},{2,1},{3,2},{4,7},{5,4},{6,5},{7,6},{8,11},{9,8},{10,9... | collective-permute-start | bytes 32 | tf_op jit(solution)/shard_map/ppermute | solution.py:414
  3.2 0.0 collective-permute-start.2
  3.2 13.2 %collective-permute-start = (s32[1,2]{1,0:T(1,128)}, s32[1,2]{1,0:T(1,128)S(1)}, u32[]{:S(2)}, u32[]{:S(2)}) collective-permute-start(s32[1,2]{1,0:T(1,128)} %bitcast.13), channel_id=1, source_target_pairs={{1,209},{3,211},{5,213},{7,215},{9,217},{11,219},{13,221},{15,223}... | collective-permute-start | bytes 32 | tf_op jit(solution)/shard_map/ppermute | solution.py:427
  16.5 0.0 copy-start
  16.5 1.2 %copy-done = f32[1,4,4,128,128]{4,3,2,1,0:T(8,128)S(1)} copy-done((f32[1,4,4,128,128]{4,3,2,1,0:T(8,128)S(1)}, f32[1,4,4,128,128]{4,3,2,1,0:T(8,128)}, u32[]{:S(2)}) %copy-start) | copy-done | bytes 1048600
  17.7 0.1 chunks.1.chunks_ref
  17.8 0.0 collective-permute-done
  17.8 2.3 %collective-permute-start.1 = (s32[1,2]{1,0:T(1,128)S(1)}, s32[1,2]{1,0:T(1,128)S(1)}, u32[]{:S(2)}, u32[]{:S(2)}) collective-permute-start(s32[1,2]{1,0:T(1,128)S(1)} %collective-permute-done), channel_id=1, source_target_pairs={{1,3},{3,1},{5,7},{7,5},{9,11},{11,9},{13,15},{15,13},{17,19},{19,... | collective-permute-start | bytes 32 | tf_op jit(solution)/shard_map/ppermute | solution.py:428
  20.1 0.0 collective-permute-done.3.right_ref
  20.1 0.0 collective-permute-done.2.left_ref
  20.1 1.9 %collective-permute-done.1.turn_ref = s32[1,2]{1,0:T(1,128)S(1)} collective-permute-done((s32[1,2]{1,0:T(1,128)S(1)}, s32[1,2]{1,0:T(1,128)S(1)}, u32[]{:S(2)}, u32[]{:S(2)}) %collective-permute-start.1) | collective-permute-done | bytes 40 | tf_op jit(solution)/shard_map/ppermute | solution.py:428
  22.1 0.0 copy-done.3
  22.1 0.1 table.1
  22.2 31.7 %all_to_all.10 = f32[64,33,1,128]{3,2,1,0:T(1,128)S(1)} all-to-all(f32[64,33,1,128]{3,2,1,0:T(1,128)S(1)} %bitcast.6), channel_id=1, replica_groups=mesh['dom'=64,'lon'=4] {'dom'}, dimensions={0} | all-to-all | bytes 2162688 | tf_op jit(solution)/shard_map/all_to_all | solution.py:440
  53.9 0.9 %blend.1 = f32[64,32,128]{2,1,0:T(8,128)S(1)} custom-call(f32[2112,128]{1,0:T(8,128)S(1)} %bitcast.9), custom_call_target="tpu_custom_call" | custom-call | flops 1081344 | bytes 2162688 | tf_op jit(solution)/shard_map/blend/pallas_call | solution.py:140
  54.8 0.0 copy-start.1
  54.8 0.0 copy-start.2
  54.9 25.7 %all_to_all.11 = f32[64,32,128]{2,1,0:T(8,128)S(1)} all-to-all(f32[64,32,128]{2,1,0:T(8,128)S(1)} %blend.1), channel_id=1, replica_groups=mesh['dom'=64,'lon'=4] {'dom'}, dimensions={0} | all-to-all | bytes 2097152 | tf_op jit(solution)/shard_map/all_to_all | solution.py:442
  80.6 0.0 copy-done.1
  80.6 0.0 copy-done.2
  80.6 0.4 pack.1
  81.0 0.1 collective-permute-start.4
  81.1 0.5 collective-permute-start.5
  81.6 2.3 %inner.1 = (f32[16,128,128]{2,1,0:T(8,128)S(1)}, f32[10,128,128]{2,1,0:T(8,128)S(1)}) custom-call(f32[16,128,128]{2,1,0:T(8,128)S(1)} %bitcast.8, f32[4,128,128]{2,1,0:T(8,128)S(1)} %copy-done.1, s32[128,128]{1,0:T(8,128)S(1)} %copy-done.2), custom_call_target="tpu_custom_call" | custom-call | flops 19660800 | bytes 3145728 | tf_op jit(solution)/shard_map/inner/pallas_call | solution.py:340
  83.8 0.0 collective-permute-done.4.before_ref
  83.9 1.0 %collective-permute-done.5.after_ref = f32[128,128]{1,0:T(8,128)S(1)} collective-permute-done((f32[128,128]{1,0:T(8,128)S(1)}, f32[128,128]{1,0:T(8,128)S(1)}, u32[]{:S(2)}, u32[]{:S(2)}) %collective-permute-start.5) | collective-permute-done | bytes 65568 | tf_op jit(solution)/shard_map/ppermute | solution.py:414
  84.8 2.6 %ends.1 = f32[16,128,128]{2,1,0:T(8,128)} custom-call(f32[16,128,128]{2,1,0:T(8,128)S(1)} %get-tuple-element.9.inner_ref, f32[10,128,128]{2,1,0:T(8,128)S(1)} %get-tuple-element.10.strip_ref, f32[128,128]{1,0:T(8,128)S(1)} %collective-permute-done.4.before_ref, f32[128,128]{1,0:T(8,128)S(1)} %collective-permute-done.5.after_ref), custom_call_target="tpu_custom_call" | custom-call | flops 10485760 | bytes 3145728 | tf_op jit(solution)/shard_map/ends/pallas_call | solution.py:395
Async XLA Ops:
  0.0 22.1 %copy-start.3 = (s32[1,2,1]{1,2,0:T(1,128)S(1)}, s32[1,2,1]{1,2,0:T(1,128)}, u32[]{:S(2)}) copy-start(s32[1,2,1]{1,2,0:T(1,128)} %param.7) | copy-start | bytes 28
  0.0 20.1 %collective-permute-start.3 = (s32[1,2]{1,0:T(1,128)}, s32[1,2]{1,0:T(1,128)S(1)}, u32[]{:S(2)}, u32[]{:S(2)}) collective-permute-start(s32[1,2]{1,0:T(1,128)} %bitcast.11), channel_id=1, source_target_pairs={{0,3},{1,0},{2,1},{3,2},{4,7},{5,4},{6,5},{7,6},{8,11},{9,8},{10,9... | collective-permute-start | bytes 32 | tf_op jit(solution)/shard_map/ppermute | solution.py:414
  3.2 16.9 %collective-permute-start.2 = (s32[1,2]{1,0:T(1,128)}, s32[1,2]{1,0:T(1,128)S(1)}, u32[]{:S(2)}, u32[]{:S(2)}) collective-permute-start(s32[1,2]{1,0:T(1,128)} %bitcast.12), channel_id=1, source_target_pairs={{0,1},{1,2},{2,3},{3,0},{4,5},{5,6},{6,7},{7,4},{8,9},{9,10},{10,1... | collective-permute-start | bytes 32 | tf_op jit(solution)/shard_map/ppermute | solution.py:414
  3.2 14.5 %collective-permute-start = (s32[1,2]{1,0:T(1,128)}, s32[1,2]{1,0:T(1,128)S(1)}, u32[]{:S(2)}, u32[]{:S(2)}) collective-permute-start(s32[1,2]{1,0:T(1,128)} %bitcast.13), channel_id=1, source_target_pairs={{1,209},{3,211},{5,213},{7,215},{9,217},{11,219},{13,221},{15,223}... | collective-permute-start | bytes 32 | tf_op jit(solution)/shard_map/ppermute | solution.py:427
  16.5 1.2 %copy-start = (f32[1,4,4,128,128]{4,3,2,1,0:T(8,128)S(1)}, f32[1,4,4,128,128]{4,3,2,1,0:T(8,128)}, u32[]{:S(2)}) copy-start(f32[1,4,4,128,128]{4,3,2,1,0:T(8,128)} %param.4) | copy-start | bytes 3145732
  17.8 4.3 %collective-permute-start.1 = (s32[1,2]{1,0:T(1,128)S(1)}, s32[1,2]{1,0:T(1,128)S(1)}, u32[]{:S(2)}, u32[]{:S(2)}) collective-permute-start(s32[1,2]{1,0:T(1,128)S(1)} %collective-permute-done), channel_id=1, source_target_pairs={{1,3},{3,1},{5,7},{7,5},{9,11},{11,9},{13,15},{15,13},{17,19},{19,... | collective-permute-start | bytes 32 | tf_op jit(solution)/shard_map/ppermute | solution.py:428
  54.8 25.7 %copy-start.1 = (f32[4,128,128]{2,1,0:T(8,128)S(1)}, f32[4,128,128]{2,1,0:T(8,128)}, u32[]{:S(2)}) copy-start(f32[4,128,128]{2,1,0:T(8,128)} %depth_ref.3) | copy-start | bytes 786436
  54.8 25.7 %copy-start.2 = (s32[128,128]{1,0:T(8,128)S(1)}, s32[128,128]{1,0:T(8,128)}, u32[]{:S(2)}) copy-start(s32[128,128]{1,0:T(8,128)} %levels_ref.3) | copy-start | bytes 196612
  81.0 2.9 %collective-permute-start.4 = (f32[128,128]{1,0:T(8,128)S(1)}, f32[128,128]{1,0:T(8,128)S(1)}, u32[]{:S(2)}, u32[]{:S(2)}) collective-permute-start(f32[128,128]{1,0:T(8,128)S(1)} %get-tuple-element.11), channel_id=1, source_target_pairs={{0,1},{1,2},{2,3},{3,0},{4,5},{5,6},{6,7},{7,4},{8,9},{9,10},{10,1... | collective-permute-start | bytes 196616 | tf_op jit(solution)/shard_map/ppermute | solution.py:414
  81.1 3.8 %collective-permute-start.5 = (f32[128,128]{1,0:T(8,128)S(1)}, f32[128,128]{1,0:T(8,128)S(1)}, u32[]{:S(2)}, u32[]{:S(2)}) collective-permute-start(f32[128,128]{1,0:T(8,128)S(1)} %get-tuple-element.12), channel_id=1, source_target_pairs={{0,3},{1,0},{2,1},{3,2},{4,7},{5,4},{6,5},{7,6},{8,11},{9,8},{10,9... | collective-permute-start | bytes 196616 | tf_op jit(solution)/shard_map/ppermute | solution.py:414
